TPU v7x, 128 devices: a whole 4x4x4 slice. The times are simulated.
128 devices in a mesh: tm: 4 (over y), chan: 32 (over z, x, core).
Axes of the slice: x: 4, y: 4, z: 4, core: 2. Of those that a mesh axis runs over, the one named last changes fastest.
Arguments:
- raw_traces: float32 [8192, 32768], P(None, ('tm', 'chan'))
- fir_taps: float32 [129], replicated, may hold values from -0.5 to 0.5
- chan_order: int32 [8192], replicated, may hold values from 0 to 8191, each once
- vs_index: int32 [64], replicated, may hold values from 0 to 8191
Outputs:
- stacked: float32 [64, 8192, 1024], P('tm', 'chan')
Inputs may be any that keep to these rules, and one draw needn't show every extreme that they name: `chan_order`: each of the 8192 positions names a different acquisition channel.
All inputs are finite; a program needn't handle non-finite values.
Results may differ from a plain program's by a relative error of at most 0.022.
Values may be sent and summed in bfloat16 or wider, within the bound.
A program may use at most 192 MiB of HBM per device.

v0:
```python
import math

import jax
import jax.numpy as jnp
from jax import lax
from jax.sharding import PartitionSpec as P

NF = 1024
NB = 128
K0 = 4
WS = 8


exact_mode = lax.Precision.HIGHEST


def padded_2(block, sides, width):
    for axis, dim in sides:
        count = lax.axis_size(axis)
        forward = [(i, i + 1) for i in range(count - 1)]
        backward = [(target, source) for source, target in forward]
        low = lax.ppermute(
            lax.slice_in_dim(block, block.shape[dim] - width, None, axis=dim), axis, forward
        )
        high = lax.ppermute(lax.slice_in_dim(block, 0, width, axis=dim), axis, backward)
        block = jnp.concatenate([low, block, high], axis=dim)
    return block


def transform_tables(length, band_bins, lowest_frequency):
    bin_index = jnp.arange(band_bins, dtype=jnp.int32)[:, None] + lowest_frequency
    sample_index = jnp.arange(length, dtype=jnp.int32)[None, :]
    phase_index = (bin_index * sample_index % length).astype(jnp.float32) * (2.0 * math.pi / length)
    forward = jnp.concatenate([jnp.cos(phase_index), -jnp.sin(phase_index)], 0) / math.sqrt(length)
    lag_phase = (bin_index * (sample_index - length // 2) % length).astype(jnp.float32) * (
        2.0 * math.pi / length
    )
    inverse = jnp.concatenate([jnp.cos(lag_phase), -jnp.sin(lag_phase)], 0)
    return (forward, inverse)


def smoothing(band_bins, reach):
    row_bins = jnp.arange(band_bins, dtype=jnp.int32)[:, None]
    col_bins = jnp.arange(band_bins, dtype=jnp.int32)[None, :]
    nearby = (jnp.abs(row_bins - col_bins) <= reach).astype(jnp.float32)
    return nearby / jnp.sum(nearby, 1, keepdims=True)


def filter_rows(padded, fir_taps):
    block_width = fir_taps.shape[0] - 1
    rows_idx = jnp.arange(block_width, dtype=jnp.int32)[:, None]
    cols_idx = jnp.arange(2 * block_width, dtype=jnp.int32)[None, :]
    offset = cols_idx - rows_idx
    kernel = jnp.where(
        (offset >= 0) & (offset <= block_width),
        fir_taps[jnp.clip(offset, 0, block_width)],
        jnp.zeros((), fir_taps.dtype),
    )
    channel_count = padded.shape[0]
    blocks = padded.reshape(channel_count, padded.shape[1] // block_width, block_width)
    first_part = jnp.einsum(
        "rm,cbm->cbr", kernel[:, :block_width], blocks[:, :-1], precision=exact_mode
    )
    second = jnp.einsum("rm,cbm->cbr", kernel[:, block_width:], blocks[:, 1:], precision=exact_mode)
    return (first_part + second).reshape(channel_count, -1)


def clip_energy(filtered, energy, sample_total):
    root_mean = jnp.sqrt(energy / sample_total + 1e-06)[:, None]
    return jnp.clip(filtered, -2.0 * root_mean, 2.0 * root_mean)


def whiten(spectra, smoother):
    band_bins = smoother.shape[0]
    real_rows = spectra[:, :band_bins]
    imag_rows = spectra[:, band_bins:]
    power_bins = real_rows * real_rows + imag_rows * imag_rows
    smooth = jnp.einsum("jk,skc->sjc", smoother, power_bins, precision=exact_mode)
    level_mean = jnp.mean(power_bins, axis=1, keepdims=True)
    scale_bins = 1.0 / jnp.sqrt(smooth + 0.1 * level_mean + 1e-06)
    return jnp.concatenate([real_rows * scale_bins, imag_rows * scale_bins], 1).astype(jnp.bfloat16)


def cross_spectra(sources, channels):
    band_bins = sources.shape[-2] // 2
    src_real = sources[..., :band_bins, :]
    src_imag = sources[..., band_bins:, :]
    chan_real = channels[..., :band_bins, :]
    chan_imag = channels[..., band_bins:, :]
    layout_kind = "...yhz,...yhm->...zhm"
    real_part = jnp.einsum(
        layout_kind, src_real, chan_real, preferred_element_type=jnp.float32
    ) + jnp.einsum(layout_kind, src_imag, chan_imag, preferred_element_type=jnp.float32)
    imag_part = jnp.einsum(
        layout_kind, src_real, chan_imag, preferred_element_type=jnp.float32
    ) - jnp.einsum(layout_kind, src_imag, chan_real, preferred_element_type=jnp.float32)
    return jnp.concatenate([real_part, imag_part], axis=-2)


def on_device(raw_traces, fir_taps, chan_order, vs_index):
    forward, inverse = transform_tables(NF, NB, K0)
    smoother = smoothing(NB, WS)
    half_window_width = (fir_taps.shape[0] - 1) // 2
    tm_count = lax.axis_size("tm")
    chan_count = lax.axis_size("chan")
    all_chans = raw_traces.shape[0]
    slab_cols = raw_traces.shape[1]
    block_chans = all_chans // chan_count
    sample_total = slab_cols * tm_count * chan_count
    permuted = jnp.take(raw_traces, chan_order, axis=0)
    chan_block = lax.all_to_all(
        permuted.astype(jnp.bfloat16), "chan", split_axis=0, concat_axis=1, tiled=True
    ).astype(permuted.dtype)
    padded = padded_2(chan_block.astype(jnp.bfloat16), (("tm", 1),), half_window_width).astype(
        chan_block.dtype
    )
    filtered = filter_rows(padded, fir_taps)
    energy = lax.psum(jnp.sum(filtered * filtered, 1), "tm")
    clipped = clip_energy(filtered, energy, sample_total)
    spectra = jnp.einsum(
        "kn,csn->skc", forward, clipped.reshape(block_chans, -1, NF), precision=exact_mode
    )
    whitened_spectrum = whiten(spectra, smoother)
    window_segment_count = whitened_spectrum.shape[0]
    positions = lax.axis_index("chan") * block_chans + jnp.arange(block_chans, dtype=jnp.int32)
    source_selector = (vs_index[:, None] == positions[None, :]).astype(jnp.bfloat16)
    resident_sources = jnp.einsum(
        "euj,aj->eua", whitened_spectrum, source_selector, preferred_element_type=jnp.float32
    )
    sources = lax.psum(resident_sources.astype(jnp.bfloat16), "chan")
    stacked_sum = lax.psum_scatter(
        cross_spectra(sources, whitened_spectrum).astype(jnp.bfloat16),
        "tm",
        scatter_dimension=0,
        tiled=True,
    ).astype(jnp.float32)
    scale_out = 1.0 / math.sqrt(window_segment_count * tm_count * NB)
    return jnp.einsum("vkc,kl->vcl", stacked_sum, inverse, precision=exact_mode) * scale_out


def solution(mesh):
    in_specs = (P(None, ("tm", "chan")), P(), P(), P())
    out_specs = P("tm", "chan", None)
    return jax.shard_map(
        on_device, mesh=mesh, in_specs=in_specs, out_specs=out_specs, check_vma=False
    )
```

profile of v0, /device:TPU:2, one launch (start us, length us, event | category | flops | bytes accessed | tf_op | source)
XLA Modules:
  0.0 609.3 jit_solution(11432122044602361557)
XLA Ops:
  6.5 0.0 copy-start
  6.5 0.8 compare_and_fusion
  7.3 0.8 fusion.57
  8.1 34.5 %gather_fusion = bf16[8192,256]{1,0:T(8,128)(2,1)} fusion(f32[8192,256]{1,0:T(8,128)} %param.4, s32[8192]{0:T(1024)S(1)} %fusion.57), kind=kCustom, calls=%fused_computation | custom fusion | bytes 8421376 | tf_op jit(solution)/shard_map/jit(_take)/gather | solution.py:110
  42.6 6.5 %copy.6 = bf16[32,256,256]{1,2,0:T(8,128)(2,1)} copy(bf16[32,256,256]{2,1,0:T(8,128)(2,1)} %bitcast.50) | data formatting | bytes 8388608 | tf_op jit(solution)/shard_map/jit(_take)/gather | solution.py:110
  49.1 5.3 select_convert_fusion
  54.4 8.5 %all-to-all-start = ((bf16[32,256,256]{1,2,0:T(8,128)(2,1)}), bf16[32,256,256]{1,2,0:T(8,128)(2,1)}, u32[]{:S(2)}, u32[]{:S(2)}) async-start(bf16[32,256,256]{1,2,0:T(8,128)(2,1)} %select_convert_fusion), calls=%async_computation | async-start | bytes 8388608 | tf_op jit(solution)/shard_map/all_to_all | solution.py:111
  63.0 0.0 all-reduce.2.cloned.1.call-start
  63.1 0.1 copy.20
  63.2 0.0 copy-done
  63.2 203.2 %gather_fusion.1 = f32[32768]{0:T(1024)S(1)} fusion(f32[129]{0:T(256)S(1)} %copy-done, s32[32768]{0:T(1024)S(1)} %broadcast_clamp_fusion), kind=kCustom, calls=%fused_computation.1 | custom fusion | bytes 393216 | tf_op jit(solution)/shard_map/gather | solution.py:56
  266.5 4.2 fusion.41
  270.6 0.0 all-to-all-done
  270.7 0.8 fusion.63
  271.4 3.5 collective-permute-start
  274.9 1.8 collective-permute-start.1
  276.7 0.1 convert_reduce_fusion
  276.8 0.0 collective-permute-done
  276.8 3.9 collective-permute-done.1
  280.7 7.2 %pad_maximum_fusion.1 = bf16[256,8320]{0,1:T(8,128)(2,1)S(1)} fusion(bf16[256,64]{0,1:T(8,128)(2,1)S(1)} %collective-permute-done.1, bf16[256,8192]{0,1:T(8,128)(2,1)} %bitcast.2, bf16[256,64]{0,1:T(8,128)(2,1)S(1)} %collective-permute-done), kind=kLoop, calls=%fused_computation.11 | loop fusion | flops 12779520 | bytes 8519680 | tf_op jit(solution)/shard_map/concatenate | solution.py:26
  287.9 3.5 fusion.50
  291.4 7.5 %multiply_reduce_fusion = (f32[256]{0:T(256)S(1)}, f32[256,64,128]{0,2,1:T(8,128)}) fusion(f32[256,64,128]{0,2,1:T(8,128)S(1)} %fusion.50, bf16[256,65,128]{0,2,1:T(8,128)(2,1)S(1)} %bitcast.48, f32[128,256]{1,0:T(8,128)S(1)} %fusion.47), kind=kOutput, calls=%fused_computation.9 | convolution fusion | flops 3227516672 | bytes 21103616 | tf_op jit(solution)/shard_map/rm,cbm->cbr/dot_general | solution.py:61
  298.9 9.5 %psum.14 = f32[256]{0:T(256)S(1)} all-reduce(f32[256]{0:T(256)S(1)} %get-tuple-element.17), channel_id=1, replica_groups=mesh['tm'=4,'chan'=32] {'tm'}, use_global_device_ids=true, to_apply=%region_1.2 | all-reduce | flops 256 | bytes 2048 | tf_op jit(solution)/shard_map/psum | solution.py:118
  308.3 9.1 %copy.9 = f32[256,8,1024]{2,0,1:T(8,128)} copy(f32[256,8,1024]{0,2,1:T(8,128)} %bitcast.49) | data formatting | bytes 16777216 | tf_op jit(solution)/shard_map/reshape | solution.py:65
  317.5 10.7 %fusion.7 = f32[8,256,256]{2,1,0:T(8,128)S(1)} fusion(f32[256,8,1024]{2,0,1:T(8,128)} %copy.9, f32[256]{0:T(256)S(1)} %get-tuple-element.14, f32[256]{0:T(256)S(1)} %get-tuple-element.13, f32[128,1024]{1,0:T(8,128)S(1)} %get-tuple-element.15, f32[128,1024]{1,0:T(8,128)S(1)} %get-tuple-element.16), kind=kOutput, calls=%fused_computation.17 | convolution fusion | flops 6447169536 | bytes 11536384 | tf_op jit(solution)/shard_map/kn,csn->skc/dot_general | solution.py:120
  328.2 0.2 fusion.42
  328.4 1.5 multiply_convert_fusion.1
  329.8 0.0 copy-done.2
  329.8 1.2 convolution_convert_fusion
  331.0 0.0 all-reduce.2.cloned.1.call-update
  331.0 0.0 reduce-scatter.2.cloned.1.call-start
  331.1 100.0 %all-reduce.2.cloned.1.call-done = bf16[8,256,64]{1,2,0:T(8,128)(2,1)} async-done(((bf16[8,256,64]{1,2,0:T(8,128)(2,1)}), bf16[8,256,64]{1,2,0:T(8,128)(2,1)}) %all-reduce.2.cloned.1.call-update) | async-done | bytes 262160 | tf_op jit(solution)/shard_map/psum | solution.py:130
  431.0 1.0 fusion.64
  432.0 0.2 copy.14
  432.2 4.5 fusion.34
  436.7 4.5 fusion.36
  441.3 0.2 copy.11
  441.5 4.5 fusion.32
  446.0 4.7 fusion.38
  450.7 9.5 %copy.16 = f32[128,256,64]{0,1,2:T(8,128)} copy(f32[128,256,64]{1,2,0:T(8,128)} %fusion.32) | data formatting | bytes 16777216 | tf_op jit(solution)/shard_map/...yhz,...yhm->...zhm/dot_general | solution.py:94
  460.1 9.3 %copy.15 = f32[128,256,64]{0,1,2:T(8,128)} copy(f32[128,256,64]{1,2,0:T(8,128)} %fusion.34) | data formatting | bytes 16777216 | tf_op jit(solution)/shard_map/...yhz,...yhm->...zhm/dot_general | solution.py:93
  469.4 9.3 %copy.17 = f32[128,256,64]{0,1,2:T(8,128)} copy(f32[128,256,64]{1,2,0:T(8,128)} %fusion.36) | data formatting | bytes 16777216 | tf_op jit(solution)/shard_map/...yhz,...yhm->...zhm/dot_general | solution.py:96
  478.7 9.3 %copy.12 = f32[128,256,64]{0,1,2:T(8,128)} copy(f32[128,256,64]{1,2,0:T(8,128)} %fusion.38) | data formatting | bytes 16777216 | tf_op jit(solution)/shard_map/...yhz,...yhm->...zhm/dot_general | solution.py:91
  487.9 14.5 %fusion.3 = (bf16[64,128,256]{1,2,0:T(8,128)(2,1)S(1)}, bf16[64,128,256]{1,2,0:T(8,128)(2,1)}) fusion(f32[128,256,64]{0,1,2:T(8,128)} %copy.12, f32[128,256,64]{0,1,2:T(8,128)} %copy.15, f32[128,256,64]{0,1,2:T(8,128)} %copy.16, f32[128,256,64]{0,1,2:T(8,128)} %copy.17), kind=kLoop, calls=%fused_computation.12 | loop fusion | flops 8388608 | bytes 41943040 | tf_op jit(solution)/shard_map/add | solution.py:91
  502.5 7.0 %pad_maximum_fusion = bf16[64,256,256]{1,2,0:T(8,128)(2,1)} fusion(bf16[64,128,256]{1,2,0:T(8,128)(2,1)} %get-tuple-element.20, bf16[64,128,256]{1,2,0:T(8,128)(2,1)S(1)} %get-tuple-element.19), kind=kLoop, calls=%fused_computation.3 | loop fusion | flops 16777216 | bytes 16777216 | tf_op jit(solution)/shard_map/concatenate | solution.py:97
  509.5 0.0 reduce-scatter.2.cloned.1.call-update
  509.5 80.7 %reduce-scatter.2.cloned.1.call-done = bf16[16,256,256]{1,2,0:T(8,128)(2,1)} async-done(((bf16[64,256,256]{1,2,0:T(8,128)(2,1)}), bf16[16,256,256]{1,2,0:T(8,128)(2,1)}) %reduce-scatter.2.cloned.1.call-update) | async-done | bytes 2097168 | tf_op jit(solution)/shard_map/reduce_scatter | solution.py:131
  590.2 12.0 %convolution_multiply_fusion = f32[16,256,1024]{2,1,0:T(8,128)} fusion(bf16[16,256,256]{1,2,0:T(8,128)(2,1)} %reduce-scatter.2.cloned.1.call-done, f32[128,1024]{1,0:T(8,128)S(1)} %get-tuple-element.12, f32[128,1024]{1,0:T(8,128)S(1)} %get-tuple-element.11), kind=kOutput, calls=%fused_computation.2 | convolution fusion | flops 12889358336 | bytes 19922944 | tf_op jit(solution)/shard_map/vkc,kl->vcl/dot_general | solution.py:138
  (13 shorter events, 0.2 us)
Async XLA Ops:
  6.5 56.6 %copy-start = (f32[129]{0:T(256)S(1)}, f32[129]{0:T(256)}, u32[]{:S(2)}) copy-start(f32[129]{0:T(256)} %param.5) | copy-start | bytes 1552
  54.4 216.2 %all-to-all-start = ((bf16[32,256,256]{1,2,0:T(8,128)(2,1)}), bf16[32,256,256]{1,2,0:T(8,128)(2,1)}, u32[]{:S(2)}, u32[]{:S(2)}) async-start(bf16[32,256,256]{1,2,0:T(8,128)(2,1)} %select_convert_fusion), calls=%async_computation | async-start | bytes 8388608 | tf_op jit(solution)/shard_map/all_to_all | solution.py:111
  63.0 368.1 %all-reduce.2.cloned.1.call-start = ((), (), s32[]{:S(2)}) async-start(), calls=%async_computation.2 | async-start | bytes 524288 | tf_op jit(solution)/shard_map/psum | solution.py:130
  271.4 5.4 collective-permute-start
  274.9 5.8 collective-permute-start.1
  317.5 12.4 %copy-start.2 = (s32[64]{0:T(128)S(1)}, s32[64]{0:T(128)}, u32[]{:S(2)}) copy-start(s32[64]{0:T(128)} %param.7) | copy-start | bytes 772
  331.0 259.2 %reduce-scatter.2.cloned.1.call-start = ((), (), s32[]{:S(2)}) async-start(), calls=%async_computation.3 | async-start | bytes 10485760 | tf_op jit(solution)/shard_map/reduce_scatter | solution.py:131
  590.2 12.0 %copy-start.1 = (f32[129]{0:T(256)S(1)}, f32[129]{0:T(256)}, u32[]{:S(2)}) copy-start(f32[129]{0:T(256)} %param.5) | copy-start | bytes 1552
Sparse Core Ops, SparseCore 0:
  331.1 99.8 all-reduce.1
  509.6 80.5 reduce-scatter.1
where the time goes:
time: 617 us; the launch traced here: 609 us
  local copies, waits for them, and re-layouts  293 us (47%)
  waiting for transfers between devices  185 us (30%)
  matrix products  54.5 us (9%)
  other arithmetic  40.1 us (6%)
  between operations  13.9 us (2%)
  starting transfers between devices  13.8 us (2%)
  blocking collectives  9.45 us (2%)
    gather x2, local copies, waits for them, and re-layouts, filter_rows(): fir_taps[jnp.clip(offset, 0, block_width)]  203 us
    psum x1, waiting for transfers between devices, on_device(): sources = lax.psum(resident_sources.astype(jnp.bfloat16), 'chan')  100 us
    reduce_scatter x1, waiting for transfers between devices, on_device(): lax.psum_scatter(cross_spectra(sources, whitened_spectrum).astype(jnp.bfl...  80.7 us
    gather x2, local copies, waits for them, and re-layouts, on_device(): permuted = jnp.take(raw_traces, chan_order, axis=0)  41 us
    add x1, other arithmetic, cross_spectra(): jnp.einsum(layout_kind, src_real, chan_real, preferred_element_type=jnp.f...  14.5 us
  transfers between devices with their start and end apart: 5, of which 3 were waited for; matrix products, arithmetic and copies ran while one was open for 34% of the time, Pallas kernels for 0%

commit v1 on v0

v1 whole, which is shorter than its diff:
```python
import functools
import math

import jax
import jax.numpy as jnp
import numpy as np
from jax import lax
from jax.experimental import pallas as pl
from jax.experimental.pallas import tpu as pltpu
from jax.sharding import PartitionSpec as P

NF = 1024
NB = 128
K0 = 4
WS = 8
TAPS = 129
SLAB = 256
NBLK = 32
NTM = 4
SEGS = 8
VS = 64
VPT = VS // NTM
HALF = 128
T_ALL = SLAB * NBLK * NTM
MIB = 1024 * 1024
MESH = pl.DeviceIdType.MESH
BF = jnp.bfloat16
F32 = jnp.float32


def tables():
    k = np.arange(NB, dtype=np.int64)[:, None] + K0
    n = np.arange(NF, dtype=np.int64)[None, :]
    ph = (k * n % NF) * (2.0 * math.pi / NF)
    fwd = np.concatenate([np.cos(ph), -np.sin(ph)], 0) / math.sqrt(NF)
    lag = (k * (n - NF // 2) % NF) * (2.0 * math.pi / NF)
    inv = np.concatenate([np.cos(lag), -np.sin(lag)], 0) / math.sqrt(SEGS * NTM * NB)
    near = np.abs(np.arange(NB)[:, None] - np.arange(NB)[None, :]) <= WS
    count = near.sum(1)
    grow = np.concatenate([near, np.ones((NB, NB))], 0)
    return (
        fwd.astype(np.float32),
        inv.astype(np.float32),
        grow.astype(np.float32),
        (1.0 / count).astype(np.float32),
    )


def nt(a, b):
    return lax.dot_general(a, b, (((1,), (1,)), ((), ())), preferred_element_type=F32)


def tn(a, b):
    return lax.dot_general(a, b, (((0,), (0,)), ((), ())), preferred_element_type=F32)


def nn(a, b):
    return jnp.dot(a, b, preferred_element_type=F32)


def gather_kernel(order, vs, raw, out, src, buf):
    d = pl.program_id(0)

    def body(g, carry):
        for u in range(16):
            r = g * 16 + u
            buf[pl.ds(r, 1), :] = raw[pl.ds(order[d * SLAB + r], 1), :]
        return carry

    lax.fori_loop(0, SLAB // 16, body, 0)
    out[0] = buf[...].astype(BF)

    @pl.when(d == 0)
    def _():
        def pick(g, carry):
            for u in range(16):
                r = g * 16 + u
                buf[pl.ds(r, 1), :] = raw[pl.ds(order[vs[r]], 1), :]
            return carry

        lax.fori_loop(0, VS // 16, pick, 0)
        src[...] = buf[:VS].astype(BF)


def gather(raw, order, vs):
    rows, cols = raw.shape
    return pl.pallas_call(
        gather_kernel,
        grid_spec=pltpu.PrefetchScalarGridSpec(
            num_scalar_prefetch=2,
            grid=(NBLK,),
            in_specs=[pl.BlockSpec((rows, cols), lambda d, o, v: (0, 0))],
            out_specs=[
                pl.BlockSpec((1, SLAB, cols), lambda d, o, v: (d, 0, 0)),
                pl.BlockSpec((VS, cols), lambda d, o, v: (0, 0)),
            ],
            scratch_shapes=[pltpu.VMEM((SLAB, cols), F32)],
        ),
        out_shape=[
            jax.ShapeDtypeStruct((NBLK, SLAB, cols), BF),
            jax.ShapeDtypeStruct((VS, cols), BF),
        ],
        compiler_params=pltpu.CompilerParams(vmem_limit_bytes=40 * MIB),
    )(order, vs, raw)


def spectra_kernel(
    send, srcs, taps, fwd, grow, rcol, rrow, z_out, s_out,
    recv, recvs, tt, ybuf, ysrc, pbuf, zp, sp_out, ebuf, esrc,
    a_send, a_recv, h_send, h_recv, e_send, e_recv, g_send, g_recv, l_sem,
):
    i = lax.axis_index("tm")
    c = lax.axis_index("chan")
    cz, cx, cc = c // 8, (c // 2) % 4, c % 2

    def at_shift(d, sign):
        z = lax.rem(cz + sign * (d // 8) + 4, 4)
        x = lax.rem(cx + sign * ((d // 2) % 4) + 4, 4)
        k = lax.rem(cc + d % 2, 2)
        return z * 8 + x * 2 + k

    barrier = pltpu.get_barrier_semaphore()

    def greet(d, carry):
        pl.semaphore_signal(barrier, inc=1, device_id=(i, at_shift(d, 1)), device_id_type=MESH)
        return carry

    lax.fori_loop(1, NBLK, greet, 0)
    for d in range(1, NTM):
        pl.semaphore_signal(
            barrier, inc=1, device_id=(lax.rem(i + d, NTM), c), device_id_type=MESH
        )
    pl.semaphore_wait(barrier, NBLK - 1 + NTM - 1)

    def a2a(q, d, sign):
        other = at_shift(d, sign)
        if q == 2:
            src, dst = srcs, recvs.at[1 + c]
            land = recvs.at[1 + other]
        else:
            src = send.at[other, pl.ds(q * HALF, HALF)]
            dst = recv.at[q, 1 + c]
            land = recv.at[q, 1 + other]
        if sign > 0:
            return pltpu.make_async_remote_copy(
                src_ref=src, dst_ref=dst, send_sem=a_send.at[q, d], recv_sem=a_recv.at[q, c],
                device_id=(i, other), device_id_type=MESH,
            )
        return pltpu.make_async_remote_copy(
            src_ref=src, dst_ref=land, send_sem=a_send.at[q, d], recv_sem=a_recv.at[q, other],
            device_id=(i, other), device_id_type=MESH,
        )

    def own(q):
        if q == 2:
            return pltpu.make_async_copy(srcs, recvs.at[1 + c], l_sem.at[q])
        return pltpu.make_async_copy(
            send.at[c, pl.ds(q * HALF, HALF)], recv.at[q, 1 + c], l_sem.at[q]
        )

    for q in (2, 0, 1):
        own(q).start()

        def start(d, carry, q=q):
            a2a(q, d, 1).start()
            return carry

        lax.fori_loop(1, NBLK, start, 0)

    band = jnp.broadcast_to(taps[0:1, :], (SLAB, 2 * SLAB))
    tt[...] = pltpu.roll(band, 0, 1, stride=1, stride_axis=0).astype(BF)

    def box(q):
        return recvs if q == 2 else recv.at[q]

    def halo(q, side):
        b = box(q)
        if side == 0:
            return pltpu.make_async_remote_copy(
                src_ref=b.at[NBLK, :, pl.ds(128, 128)], dst_ref=b.at[0, :, pl.ds(128, 128)],
                send_sem=h_send.at[q, 0], recv_sem=h_recv.at[q, 0],
                device_id=(lax.rem(i + 1, NTM), c), device_id_type=MESH,
            )
        return pltpu.make_async_remote_copy(
            src_ref=b.at[1, :, pl.ds(0, 128)], dst_ref=b.at[NBLK + 1, :, pl.ds(0, 128)],
            send_sem=h_send.at[q, 1], recv_sem=h_recv.at[q, 1],
            device_id=(lax.rem(i + NTM - 1, NTM), c), device_id_type=MESH,
        )

    def arrive(q):
        own(q).wait()

        def wait(d, carry):
            a2a(q, d, -1).wait_recv()
            return carry

        lax.fori_loop(1, NBLK, wait, 0)
        b = box(q)
        rows = VS if q == 2 else HALF

        @pl.when(i < NTM - 1)
        def _():
            halo(q, 0).start()

        @pl.when(i > 0)
        def _():
            halo(q, 1).start()

        @pl.when(i == 0)
        def _():
            b[0, :, pl.ds(128, 128)] = jnp.zeros((rows, 128), BF)

        @pl.when(i == NTM - 1)
        def _():
            b[NBLK + 1, :, pl.ds(0, 128)] = jnp.zeros((rows, 128), BF)

    def halos_in(q):
        @pl.when(i > 0)
        def _():
            halo(q, 0).wait_recv()

        @pl.when(i < NTM - 1)
        def _():
            halo(q, 1).wait_recv()

    def energy_box(q):
        return esrc if q == 2 else ebuf.at[q]

    def energy(q, d):
        other = lax.rem(i + d, NTM)
        e = energy_box(q)
        return pltpu.make_async_remote_copy(
            src_ref=e.at[i], dst_ref=e.at[i], send_sem=e_send.at[q, d], recv_sem=e_recv.at[q, i],
            device_id=(other, c), device_id_type=MESH,
        )

    def energy_in(q, d):
        other = lax.rem(i + d, NTM)
        e = energy_box(q)
        return pltpu.make_async_remote_copy(
            src_ref=e.at[other], dst_ref=e.at[other], send_sem=e_send.at[q, d],
            recv_sem=e_recv.at[q, other], device_id=(other, c), device_id_type=MESH,
        )

    def gathered(q, d, sign):
        other = lax.rem(i + d, NTM)
        slot = i if sign > 0 else other
        if q == 2:
            src = sp_out.at[:, pl.ds(other * VPT, VPT)]
            dst = s_out.at[slot]
        else:
            src = zp.at[q]
            dst = z_out.at[:, pl.ds(slot * 16, 16), pl.ds(q * HALF, HALF)]
        return pltpu.make_async_remote_copy(
            src_ref=src, dst_ref=dst, send_sem=g_send.at[q, d], recv_sem=g_recv.at[q, slot],
            device_id=(other, c), device_id_type=MESH,
        )

    def gathered_own(q):
        if q == 2:
            return pltpu.make_async_copy(
                sp_out.at[:, pl.ds(i * VPT, VPT)], s_out.at[i], l_sem.at[3 + q]
            )
        return pltpu.make_async_copy(
            zp.at[q], z_out.at[:, pl.ds(i * 16, 16), pl.ds(q * HALF, HALF)], l_sem.at[3 + q]
        )

    def send_all(q):
        gathered_own(q).start()
        for d in range(1, NTM):
            gathered(q, d, 1).start()

    def filter_sources():
        def body(g, acc):
            b = g * 8
            w = jnp.concatenate(
                [
                    recvs[pl.ds(b, 8), :, 128:].reshape(8 * VS, 128),
                    recvs[pl.ds(b + 1, 8)].reshape(8 * VS, SLAB),
                    recvs[pl.ds(b + 2, 8), :, :128].reshape(8 * VS, 128),
                ],
                1,
            )
            y = nt(w, tt[...])
            ysrc[pl.ds(b, 8)] = y.astype(BF).reshape(8, VS, SLAB)
            sq = y * y
            sq = sq[:, :128] + sq[:, 128:]
            return acc + jnp.sum(sq.reshape(8, VS, 128), 0)

        esrc[i] = lax.fori_loop(0, NBLK // 8, body, jnp.zeros((VS, 128), F32))
        for d in range(1, NTM):
            energy(2, d).start()

    def filter_channels(q):
        def body(b, acc):
            w = jnp.concatenate(
                [recv[q, b, :, 128:], recv[q, b + 1], recv[q, b + 2, :, :128]], 1
            )
            y = nt(tt[...], w)
            ybuf[q, b] = y.astype(BF)
            return acc + jnp.sum((y * y).reshape(SLAB // 8, 8, HALF), 0)

        ebuf[q, i] = lax.fori_loop(0, NBLK, body, jnp.zeros((8, HALF), F32))
        for d in range(1, NTM):
            energy(q, d).start()

    def limit(total):
        return 2.0 * jnp.sqrt(total / T_ALL + 1e-6)

    def whiten_sources():
        for d in range(1, NTM):
            energy_in(2, d).wait_recv()
        total = esrc[0] + esrc[1] + esrc[2] + esrc[3]
        top = limit(jnp.sum(total, 1, keepdims=True))

        def body(s, carry):
            parts = []
            for j in range(4):
                y = ysrc[s * 4 + j].astype(F32)
                parts.append(jnp.clip(y, -top, top).astype(BF))
            sp = nt(jnp.concatenate(parts, 1), fwd[...])
            re, im = sp[:, :NB], sp[:, NB:]
            g = nt((re * re + im * im).astype(BF), grow[...])
            scale = lax.rsqrt(g[:, :NB] * rrow[0:1, :] + g[:, NB:] * (0.1 / NB) + 1e-6)
            sp_out[s] = jnp.concatenate([re * scale, im * scale], 1).astype(BF)
            return carry

        lax.fori_loop(0, SEGS, body, 0)
        send_all(2)

    def whiten_channels(q):
        for d in range(1, NTM):
            energy_in(q, d).wait_recv()
        total = ebuf[q, 0] + ebuf[q, 1] + ebuf[q, 2] + ebuf[q, 3]
        top = limit(jnp.sum(total, 0, keepdims=True))

        def body(s, carry):
            y = ybuf[q, pl.ds(s * 4, 4)].reshape(NF, HALF).astype(F32)
            y = jnp.clip(y, -top, top).astype(BF)
            sp = nn(fwd[...], y)
            re, im = sp[:NB], sp[NB:]
            g = nn(grow[...], (re * re + im * im).astype(BF))
            scale = lax.rsqrt(g[:NB] * rcol[...] + g[NB:] * (0.1 / NB) + 1e-6)
            pbuf[pl.ds(s, NB, stride=16), :] = re * scale
            pbuf[pl.ds(8 + s, NB, stride=16), :] = im * scale
            return carry

        lax.fori_loop(0, SEGS, body, 0)
        zp[q] = pbuf[...].reshape(NB, 16, HALF).astype(BF)
        send_all(q)

    arrive(2)
    halos_in(2)
    filter_sources()
    arrive(0)
    whiten_sources()
    halos_in(0)
    filter_channels(0)
    whiten_channels(0)
    arrive(1)
    halos_in(1)
    filter_channels(1)
    whiten_channels(1)

    for q in range(3):
        gathered_own(q).wait()
        for d in range(1, NTM):
            gathered(q, d, 1).wait_send()
            gathered(q, d, -1).wait_recv()
            energy(q, d).wait_send()

        @pl.when(i < NTM - 1)
        def _():
            halo(q, 0).wait_send()

        @pl.when(i > 0)
        def _():
            halo(q, 1).wait_send()

        def sent(d, carry, q=q):
            a2a(q, d, 1).wait_send()
            return carry

        lax.fori_loop(1, NBLK, sent, 0)


def whitened_spectra(send, srcs, taps, fwd, grow, rcol, rrow):
    vm = pl.BlockSpec(memory_space=pltpu.VMEM)
    hb = pl.BlockSpec(memory_space=pl.ANY)
    dma = pltpu.SemaphoreType.DMA
    return pl.pallas_call(
        spectra_kernel,
        out_shape=[
            jax.ShapeDtypeStruct((NB, NTM * 16, SLAB), BF),
            jax.ShapeDtypeStruct((NTM, SEGS, VPT, 2 * NB), BF),
        ],
        in_specs=[hb, hb, vm, vm, vm, vm, vm],
        out_specs=[hb, hb],
        scratch_shapes=[
            pltpu.VMEM((2, NBLK + 2, HALF, SLAB), BF),
            pltpu.VMEM((NBLK + 2, VS, SLAB), BF),
            pltpu.VMEM((SLAB, 2 * SLAB), BF),
            pltpu.VMEM((2, NBLK, SLAB, HALF), BF),
            pltpu.VMEM((NBLK, VS, SLAB), BF),
            pltpu.VMEM((NB * 16, HALF), F32),
            pltpu.VMEM((2, NB, 16, HALF), BF),
            pltpu.VMEM((SEGS, VS, 2 * NB), BF),
            pltpu.VMEM((2, NTM, 8, HALF), F32),
            pltpu.VMEM((NTM, VS, 128), F32),
            dma((3, NBLK)), dma((3, NBLK)), dma((3, 2)), dma((3, 2)),
            dma((3, NTM)), dma((3, NTM)), dma((3, NTM)), dma((3, NTM)), dma((6,)),
        ],
        compiler_params=pltpu.CompilerParams(
            collective_id=0, has_side_effects=True, vmem_limit_bytes=48 * MIB
        ),
    )(send, srcs, taps, fwd, grow, rcol, rrow)


def lag_kernel(z, s, inv, out, smat, u, x):
    v = pl.program_id(1)

    @pl.when((pl.program_id(0) == 0) & (v == 0))
    def _():
        flat = s[...].reshape(NTM * SEGS * VPT, 2 * NB).astype(F32)
        smat[0] = flat[:, :NB]
        smat[1] = flat[:, NB:]
        for w in range(VPT):
            re = smat[0, pl.ds(w, NTM * SEGS, stride=VPT), :]
            im = smat[1, pl.ds(w, NTM * SEGS, stride=VPT), :]
            real, imag = [], []
            for t in range(NTM):
                r, m = re[t * SEGS : (t + 1) * SEGS], im[t * SEGS : (t + 1) * SEGS]
                real += [r, m]
                imag += [-m, r]
            both = jnp.concatenate(real + imag, 0).T
            u[pl.ds(2 * w * NB, NB), 0:64] = both[:, :64]
            u[pl.ds((2 * w + 1) * NB, NB), 0:64] = both[:, 64:]

    @pl.when(v == 0)
    def _():
        def body(g, carry):
            for j in range(8):
                k = g * 8 + j
                lhs = u[pl.ds(k, 2 * VPT, stride=NB), :][:, :64].astype(BF)
                x[pl.ds(k, 2 * VPT, stride=NB), :] = nn(lhs, z[k])
            return carry

        lax.fori_loop(0, NB // 8, body, 0)

    rows = x[pl.ds(pl.multiple_of(v * 2 * NB, 2 * NB), 2 * NB), :]
    out[0] = tn(rows.astype(BF), inv[...])


def lags(z, s, inv):
    return pl.pallas_call(
        lag_kernel,
        grid=(2, VPT),
        in_specs=[
            pl.BlockSpec((NB, NTM * 16, HALF), lambda q, v: (0, 0, q)),
            pl.BlockSpec((NTM, SEGS, VPT, 2 * NB), lambda q, v: (0, 0, 0, 0)),
            pl.BlockSpec((2 * NB, NF), lambda q, v: (0, 0)),
        ],
        out_specs=pl.BlockSpec((1, HALF, NF), lambda q, v: (v, q, 0)),
        out_shape=jax.ShapeDtypeStruct((VPT, SLAB, NF), F32),
        scratch_shapes=[
            pltpu.VMEM((2, NTM * SEGS * VPT, NB), F32),
            pltpu.VMEM((2 * VPT * NB, 128), F32),
            pltpu.VMEM((2 * VPT * NB, HALF), F32),
        ],
        compiler_params=pltpu.CompilerParams(vmem_limit_bytes=40 * MIB),
    )(z, s, inv)


def on_device(raw_traces, fir_taps, chan_order, vs_index):
    fwd, inv, grow, rcount = tables()
    send, srcs = gather(raw_traces, chan_order, vs_index)
    taps = jnp.zeros((8, 2 * SLAB), F32).at[:, 64 : 64 + TAPS].set(fir_taps[None, :])
    z, s = whitened_spectra(
        send, srcs, taps,
        jnp.asarray(fwd, BF), jnp.asarray(grow, BF),
        jnp.asarray(np.broadcast_to(rcount[:, None], (NB, HALF))),
        jnp.asarray(np.broadcast_to(rcount[None, :], (8, NB))),
    )
    return lags(z, s, jnp.asarray(inv, BF))


def solution(mesh):
    in_specs = (P(None, ("tm", "chan")), P(), P(), P())
    out_specs = P("tm", "chan", None)
    return jax.shard_map(
        on_device, mesh=mesh, in_specs=in_specs, out_specs=out_specs, check_vma=False
    )
```

time: 617 us -> 207 us (0.34)
  local copies, waits for them, and re-layouts: 293 us -> 6.97 us
  Pallas kernels: 0 us -> 194 us
  waiting for transfers between devices: 185 us -> 0 us
  matrix products: 54.5 us -> 0 us
  other arithmetic: 40.1 us -> 1.97 us
  between operations: 13.9 us -> 0.06 us
  starting transfers between devices: 13.8 us -> 0 us
  blocking collectives: 9.45 us -> 0 us
    gather x4 -> x0, local copies, waits for them, and re-layouts: 244 us -> none  [the longest x2 203 us: filter_rows(): fir_taps[jnp.clip(offset, 0, block_width)]]
    pallas_call x0 -> x3, Pallas kernels: none -> 194 us  [the longest x1 136 us: whitened_spectra(): pl.pallas_call(spectra_kernel, out_shape=[jax.ShapeDtypeStruct((NB, NTM *...]
    psum x1 -> x0, waiting for transfers between devices: 100 us -> none  [on_device(): sources = lax.psum(resident_sources.astype(jnp.bfloat16), 'chan')]
    reduce_scatter x1 -> x0, waiting for transfers between devices: 80.7 us -> none  [on_device(): lax.psum_scatter(cross_spectra(sources, whitened_spectrum).astype(jnp.bfl...]
    dot_general x10 -> x0, matrix products: 54.5 us -> none  [the longest x1 12 us: on_device(): jnp.einsum('vkc,kl->vcl', stacked_sum, inverse, precision=exact_mode)]
    dot_general x4 -> x0, local copies, waits for them, and re-layouts: 37.3 us -> none  [the longest x1 9.46 us: cross_spectra(): jnp.einsum(layout_kind, src_real, chan_imag, preferred_element_type=jnp.f...]
    add x3 -> x0, other arithmetic: 14.5 us -> none  [the longest x1 14.5 us: cross_spectra(): jnp.einsum(layout_kind, src_real, chan_real, preferred_element_type=jnp.f...]
    concatenate x2 -> x0, other arithmetic: 14.2 us -> none  [the longest x1 7.17 us: padded_2(): block = jnp.concatenate([low, block, high], axis=dim)]
  transfers between devices with their start and end apart: 5 -> 0, of which waited for: 3 -> 0; matrix products, arithmetic and copies ran while one was open for 34% -> 0% of each run, Pallas kernels for 0% -> 0%
where the time goes in v1:
time: 207 us; the launch traced here: 203 us
  Pallas kernels  194 us (94%)
  local copies, waits for them, and re-layouts  6.97 us (3%)
    pallas_call x1, Pallas kernels, whitened_spectra(): pl.pallas_call(spectra_kernel, out_shape=[jax.ShapeDtypeStruct((NB, NTM *...  136 us
    pallas_call x1, Pallas kernels, gather(): pl.pallas_call(gather_kernel, grid_spec=pltpu.PrefetchScalarGridSpec(num_...  31.5 us
    pallas_call x1, Pallas kernels, lags(): pl.pallas_call(lag_kernel, grid=(2, VPT), in_specs=[pl.BlockSpec((NB, NTM...  26.3 us
    unnamed x16, local copies, waits for them, and re-layouts  6.82 us

profile of v1, /device:TPU:2, one launch (start us, length us, event | category | flops | bytes accessed | tf_op | source)
XLA Modules:
  0.0 202.8 jit_solution(7141063857295072281)
XLA Ops:
  0.0 0.0 copy-start.7
  0.0 0.6 compare_reduce_fusion
  0.6 1.3 broadcast_select_fusion
  2.0 0.1 scatter.7
  2.1 0.0 copy-start
  2.1 3.4 %copy-done = f32[8192,256]{1,0:T(8,128)S(1)} copy-done((f32[8192,256]{1,0:T(8,128)S(1)}, f32[8192,256]{1,0:T(8,128)}, u32[]{:S(2)}) %copy-start) | copy-done | bytes 8388632
  5.4 0.0 copy-start.5
  5.4 0.8 copy-done.5
  6.2 0.0 copy-start.6
  6.2 0.7 copy-done.6
  6.9 0.0 copy-start.3
  6.9 0.0 copy-start.4
  6.9 0.0 copy-start.2
  6.9 31.5 %shard_map.91 = (bf16[32,256,256]{2,1,0:T(8,128)(2,1)S(1)}, bf16[64,256]{1,0:T(8,128)(2,1)S(1)}) custom-call(s32[8192]{0:T(1024)S(1)} %copy-done.5, s32[64]{0:T(128)S(1)} %copy-done.6, f32[8192,256]{1,0:T(8,128)S(1)} %copy-done), custom_call_target="tpu_custom_call" | custom-call | tf_op jit(solution)/shard_map/pallas_call | solution.py:87
  38.4 0.0 copy-start.1
  38.4 2.0 copy-done.1
  40.4 0.0 copy-done.7
  40.4 0.1 jit_solution_.6.rcol
  40.5 0.0 copy-done.3
  40.5 0.0 copy-done.4
  40.5 136.1 %shard_map.92 = (bf16[128,64,256]{2,1,0:T(8,128)(2,1)S(1)}, bf16[4,8,16,256]{3,2,1,0:T(8,128)(2,1)S(1)}) custom-call(bf16[32,256,256]{2,1,0:T(8,128)(2,1)} %copy-done.1, bf16[64,256]{1,0:T(8,128)(2,1)S(1)} %get-tuple-element.22.srcs, f32[8,512]{1,0:T(8,128)S(1)} %scatter.8.taps, bf16[256,1024]{1,0:T(8,128)(2,1)S(1)} %copy-done.3, ...), custom_call_target="tpu_custom_call" | custom-call | tf_op jit(solution)/shard_map/pallas_call | solution.py:391
  176.6 0.0 copy-done.2
  176.6 26.3 %shard_map.93 = f32[16,256,1024]{2,1,0:T(8,128)} custom-call(bf16[128,64,256]{2,1,0:T(8,128)(2,1)S(1)} %get-tuple-element.23.z, bf16[4,8,16,256]{3,2,1,0:T(8,128)(2,1)S(1)} %get-tuple-element.24.s, bf16[256,1024]{1,0:T(8,128)(2,1)S(1)} %copy-done.2), custom_call_target="tpu_custom_call" | custom-call | tf_op jit(solution)/shard_map/pallas_call | solution.py:455
  (2 shorter events, 0.0 us)
Async XLA Ops:
  0.0 40.4 %copy-start.7 = (f32[128]{0:T(128)S(1)}, f32[128]{0:T(128)}, u32[]{:S(2)}) copy-start(f32[128]{0:T(128)} %constant.41.clone) | copy-start | bytes 1540
  2.1 3.4 %copy-start = (f32[8192,256]{1,0:T(8,128)S(1)}, f32[8192,256]{1,0:T(8,128)}, u32[]{:S(2)}) copy-start(f32[8192,256]{1,0:T(8,128)} %raw.1) | copy-start | bytes 25165828
  5.4 0.8 copy-start.5
  6.2 0.7 copy-start.6
  6.9 33.6 %copy-start.3 = (bf16[256,1024]{1,0:T(8,128)(2,1)S(1)}, bf16[256,1024]{1,0:T(8,128)(2,1)}, u32[]{:S(2)}) copy-start(bf16[256,1024]{1,0:T(8,128)(2,1)} %constant.39.clone.fwd) | copy-start | bytes 1572868
  6.9 33.6 %copy-start.4 = (bf16[256,128]{1,0:T(8,128)(2,1)S(1)}, bf16[256,128]{1,0:T(8,128)(2,1)}, u32[]{:S(2)}) copy-start(bf16[256,128]{1,0:T(8,128)(2,1)} %constant.40.clone.grow) | copy-start | bytes 196612
  6.9 169.7 %copy-start.2 = (bf16[256,1024]{1,0:T(8,128)(2,1)S(1)}, bf16[256,1024]{1,0:T(8,128)(2,1)}, u32[]{:S(2)}) copy-start(bf16[256,1024]{1,0:T(8,128)(2,1)} %constant.42.clone.inv) | copy-start | bytes 1572868
  38.4 2.0 copy-start.1

commit v2 on v1

v2 whole, which is shorter than its diff:
```python
import functools
import math

import jax
import jax.numpy as jnp
import numpy as np
from jax import lax
from jax.experimental import pallas as pl
from jax.experimental.pallas import tpu as pltpu
from jax.sharding import PartitionSpec as P

NF = 1024
NB = 128
K0 = 4
WS = 8
TAPS = 129
SLAB = 256
NBLK = 32
NTM = 4
SEGS = 8
VS = 64
VPT = VS // NTM
HALF = 128
T_ALL = SLAB * NBLK * NTM
MIB = 1024 * 1024
MESH = pl.DeviceIdType.MESH
BF = jnp.bfloat16
F32 = jnp.float32


def tables():
    k = np.arange(NB, dtype=np.int64)[:, None] + K0
    n = np.arange(NF, dtype=np.int64)[None, :]
    ph = (k * n % NF) * (2.0 * math.pi / NF)
    fwd = np.concatenate([np.cos(ph), -np.sin(ph)], 0) / math.sqrt(NF)
    lag = (k * (n - NF // 2) % NF) * (2.0 * math.pi / NF)
    inv = np.concatenate([np.cos(lag), -np.sin(lag)], 0) / math.sqrt(SEGS * NTM * NB)
    near = np.abs(np.arange(NB)[:, None] - np.arange(NB)[None, :]) <= WS
    count = near.sum(1)
    grow = np.concatenate([near, np.ones((NB, NB))], 0)
    return (
        fwd.astype(np.float32),
        inv.astype(np.float32),
        grow.astype(np.float32),
        (1.0 / count).astype(np.float32),
    )


def nt(a, b):
    return lax.dot_general(a, b, (((1,), (1,)), ((), ())), preferred_element_type=F32)


def tn(a, b):
    return lax.dot_general(a, b, (((0,), (0,)), ((), ())), preferred_element_type=F32)


def nn(a, b):
    return jnp.dot(a, b, preferred_element_type=F32)


def spectra_kernel(
    order, vs, raw, taps, fwd, grow, rcol, rrow, xout,
    rows2, line, send, srcs, recv, recvs, tt, ybuf, ysrc, pbuf, zp, z, sp_out, sg, smat, u, x,
    ebuf, esrc, r_sem, a_send, a_recv, h_send, h_recv, e_send, e_recv, g_send, g_recv,
    s_send, s_recv,
):
    i = lax.axis_index("tm")
    c = lax.axis_index("chan")
    cz, cx, cc = c // 8, (c // 2) % 4, c % 2
    group, base = c % NTM, (c // NTM) * NTM
    up, down = lax.rem(i + 1, NTM), lax.rem(i + NTM - 1, NTM)

    def at_shift(d, sign):
        d = (d * 11) % NBLK
        z = lax.rem(cz + sign * (d // 8) + 4, 4)
        x = lax.rem(cx + sign * ((d // 2) % 4) + 4, 4)
        k = lax.rem(cc + d % 2, 2)
        return z * 8 + x * 2 + k

    def load(p):
        part = raw.shape[0] // 4
        r = pl.ds((p // 2) * part, part)
        return pltpu.make_async_copy(
            raw.at[r, pl.ds((p % 2) * 128, 128)], rows2.at[r, p % 2], r_sem.at[p]
        )

    for p in range(8):
        load(p).start()

    barrier = pltpu.get_barrier_semaphore()

    def greet(d, carry):
        pl.semaphore_signal(barrier, inc=1, device_id=(i, at_shift(d, 1)), device_id_type=MESH)
        return carry

    lax.fori_loop(1, NBLK, greet, 0)
    for d in range(1, NTM):
        pl.semaphore_signal(
            barrier, inc=1, device_id=(lax.rem(i + d, NTM), c), device_id_type=MESH
        )
    for t in range(NTM):

        @pl.when((i != t) | (group != i))
        def _():
            pl.semaphore_signal(barrier, inc=1, device_id=(t, base + i), device_id_type=MESH)

    band = jnp.broadcast_to(taps[0:1, :], (SLAB, 2 * SLAB))
    tt[...] = pltpu.roll(band, 0, 1, stride=1, stride_axis=0).astype(BF)

    for p in range(8):
        load(p).wait()
    peers = NBLK - 1 + NTM - 1 + NTM

    @pl.when(group == i)
    def _():
        pl.semaphore_wait(barrier, peers - 1)

    @pl.when(group != i)
    def _():
        pl.semaphore_wait(barrier, peers)

    def a2a(q, d, sign):
        other = at_shift(d, sign)
        owner = c if sign > 0 else other
        if q == 2:
            src, dst = srcs.at[pl.ds((other % NTM) * VPT, VPT)], recvs.at[1 + owner]
        else:
            src, dst = send.at[q, d], recv.at[q, 1 + owner]
        return pltpu.make_async_remote_copy(
            src_ref=src, dst_ref=dst, send_sem=a_send.at[q, d], recv_sem=a_recv.at[q, owner],
            device_id=(i, other), device_id_type=MESH,
        )

    def fetch(count, position):
        def body(g, carry):
            for t in range(64):
                r = g * 64 + t
                line[pl.ds(pl.multiple_of(2 * r, 2), 2), :] = rows2[position(r)]
            return carry

        lax.fori_loop(0, count // 64, body, 0)
        return [line[pl.ds(h, count, stride=2), :].astype(BF) for h in range(2)]

    lo, hi = fetch(VS, lambda r: order[vs[r]])
    srcs[:, 0:128] = lo
    srcs[:, 128:256] = hi

    def send_sources(d, carry):
        a2a(2, d, 1).start()
        return carry

    lax.fori_loop(1, NBLK, send_sources, 0)
    recvs[1 + c] = srcs[pl.ds(pl.multiple_of(group * VPT, VPT), VPT)]

    def send_channels(q):
        lo, hi = fetch(HALF, lambda r: order[c * SLAB + q * HALF + r])
        recv[q, 1 + c, :, 0:128] = lo
        recv[q, 1 + c, :, 128:256] = hi

        def body(d, carry):
            start = at_shift(d, 1) * SLAB + q * HALF
            lo, hi = fetch(HALF, lambda r: order[start + r])
            send[q, d, :, 0:128] = lo
            send[q, d, :, 128:256] = hi
            if q == 1:
                a2a(0, d, 1).wait_send()
            a2a(q, d, 1).start()
            return carry

        lax.fori_loop(1, NBLK, body, 0)

    def box(q):
        return recvs if q == 2 else recv.at[q]

    def halo(q, side):
        b = box(q)
        if side == 0:
            return pltpu.make_async_remote_copy(
                src_ref=b.at[NBLK, :, pl.ds(128, 128)], dst_ref=b.at[0, :, pl.ds(128, 128)],
                send_sem=h_send.at[q, 0], recv_sem=h_recv.at[q, 0],
                device_id=(up, c), device_id_type=MESH,
            )
        return pltpu.make_async_remote_copy(
            src_ref=b.at[1, :, pl.ds(0, 128)], dst_ref=b.at[NBLK + 1, :, pl.ds(0, 128)],
            send_sem=h_send.at[q, 1], recv_sem=h_recv.at[q, 1],
            device_id=(down, c), device_id_type=MESH,
        )

    def arrive(q):
        def wait(d, carry):
            a2a(q, d, -1).wait_recv()
            return carry

        lax.fori_loop(1, NBLK, wait, 0)
        b = box(q)
        rows = VPT if q == 2 else HALF

        @pl.when(i < NTM - 1)
        def _():
            halo(q, 0).start()

        @pl.when(i > 0)
        def _():
            halo(q, 1).start()

        @pl.when(i == 0)
        def _():
            b[0, :, pl.ds(128, 128)] = jnp.zeros((rows, 128), BF)

        @pl.when(i == NTM - 1)
        def _():
            b[NBLK + 1, :, pl.ds(0, 128)] = jnp.zeros((rows, 128), BF)

    def halos_in(q):
        @pl.when(i > 0)
        def _():
            halo(q, 0).wait_recv()

        @pl.when(i < NTM - 1)
        def _():
            halo(q, 1).wait_recv()

    def energy(q, d, sign):
        other = lax.rem(i + d, NTM)
        owner = i if sign > 0 else other
        e = esrc if q == 2 else ebuf.at[q]
        return pltpu.make_async_remote_copy(
            src_ref=e.at[owner], dst_ref=e.at[owner], send_sem=e_send.at[q, d],
            recv_sem=e_recv.at[q, owner], device_id=(other, c), device_id_type=MESH,
        )

    def block(q, h, owner):
        return z.at[pl.ds(h * 64, 64), pl.ds(owner * 16, 16), pl.ds(q * HALF, HALF)]

    def direct(q, h, way):
        return pltpu.make_async_remote_copy(
            src_ref=zp.at[q, pl.ds(h * 64, 64)], dst_ref=block(q, h, i),
            send_sem=g_send.at[q, h, way], recv_sem=g_recv.at[q, h, i],
            device_id=(up if way == 0 else down, c), device_id_type=MESH,
        )

    def forward(q, h):
        owner = down if h == 0 else up
        return pltpu.make_async_remote_copy(
            src_ref=block(q, h, owner), dst_ref=block(q, h, owner),
            send_sem=g_send.at[q, h, 2], recv_sem=g_recv.at[q, h, owner],
            device_id=(up if h == 0 else down, c), device_id_type=MESH,
        )

    def landed(q, h, owner):
        return pltpu.make_async_remote_copy(
            src_ref=block(q, h, owner), dst_ref=block(q, h, owner),
            send_sem=g_send.at[q, h, 2], recv_sem=g_recv.at[q, h, owner],
            device_id=(up, c), device_id_type=MESH,
        )

    def spread(q):
        for h in range(2):
            direct(q, h, h).start()
        for h in range(2):
            direct(q, h, 1 - h).start()
        z[:, pl.ds(pl.multiple_of(i * 16, 16), 16), q * HALF : (q + 1) * HALF] = zp[q]

    def pass_on(q):
        for h in range(2):
            landed(q, h, down if h == 0 else up).wait_recv()
            forward(q, h).start()

    def collect(q):
        for h in range(2):
            landed(q, h, up if h == 0 else down).wait_recv()
            landed(q, h, lax.rem(i + 2, NTM)).wait_recv()

    def filter_sources():
        w = jnp.concatenate(
            [
                recvs[0:NBLK, :, 128:].reshape(NBLK * VPT, 128),
                recvs[1 : NBLK + 1].reshape(NBLK * VPT, SLAB),
                recvs[2 : NBLK + 2, :, :128].reshape(NBLK * VPT, 128),
            ],
            1,
        )
        y = nt(w, tt[...])
        ysrc[...] = y.astype(BF).reshape(NBLK, VPT, SLAB)
        sq = y * y
        sq = sq[:, :128] + sq[:, 128:]
        esrc[i] = jnp.sum(sq.reshape(NBLK, VPT, 128), 0)
        for d in range(1, NTM):
            energy(2, d, 1).start()

    def filter_channels(q):
        def body(g, acc):
            b = g * 4
            w = jnp.concatenate(
                [
                    recv[q, pl.ds(b, 4), :, 128:].reshape(4 * HALF, 128),
                    recv[q, pl.ds(b + 1, 4)].reshape(4 * HALF, SLAB),
                    recv[q, pl.ds(b + 2, 4), :, :128].reshape(4 * HALF, 128),
                ],
                1,
            )
            y = nt(w, tt[...])
            ybuf[pl.ds(b, 4)] = y.astype(BF).reshape(4, HALF, SLAB)
            sq = y * y
            sq = sq[:, :128] + sq[:, 128:]
            return acc + jnp.sum(sq.reshape(4, HALF, 128), 0)

        acc = lax.fori_loop(0, NBLK // 4, body, jnp.zeros((HALF, 128), F32))
        ebuf[q, i] = jnp.sum(acc.T.reshape(16, 8, HALF), 0)
        for d in range(1, NTM):
            energy(q, d, 1).start()

    def limit(total):
        return 2.0 * jnp.sqrt(total / T_ALL + 1e-6)

    def source_copy(e):
        return pltpu.make_async_remote_copy(
            src_ref=sp_out, dst_ref=sg.at[i], send_sem=s_send.at[e], recv_sem=s_recv.at[i],
            device_id=(group, base + e), device_id_type=MESH,
        )

    def source_landed(t):
        return pltpu.make_async_remote_copy(
            src_ref=sp_out, dst_ref=sg.at[t], send_sem=s_send.at[0], recv_sem=s_recv.at[t],
            device_id=(t, base + i), device_id_type=MESH,
        )

    def whiten_sources():
        for d in range(1, NTM):
            energy(2, d, -1).wait_recv()
        total = esrc[0] + esrc[1] + esrc[2] + esrc[3]
        top = limit(jnp.sum(total, 1, keepdims=True))
        top = jnp.broadcast_to(top[None], (SEGS, VPT, 1)).reshape(SEGS * VPT, 1)
        parts = []
        for j in range(4):
            y = jnp.concatenate([ysrc[s * 4 + j] for s in range(SEGS)], 0).astype(F32)
            parts.append(jnp.clip(y, -top, top).astype(BF))
        sp = nt(jnp.concatenate(parts, 1), fwd[...])
        re, im = sp[:, :NB], sp[:, NB:]
        g = nt((re * re + im * im).astype(BF), grow[...])
        scale = lax.rsqrt(g[:, :NB] * rrow[0:1, :] + g[:, NB:] * (0.1 / NB) + 1e-6)
        white = jnp.concatenate([re * scale, im * scale], 1).astype(BF)
        sp_out[...] = white.reshape(SEGS, VPT, 2 * NB)
        for e in range(NTM):

            @pl.when((group != i) | (group != e))
            def _():
                source_copy(e).start()

        @pl.when(group == i)
        def _():
            sg[i] = sp_out[...]

    def sources_in():
        for t in range(NTM):

            @pl.when((i != t) | (group != i))
            def _():
                source_landed(t).wait_recv()

        flat = sg[...].reshape(NTM * SEGS * VPT, 2 * NB).astype(F32)
        smat[0] = flat[:, :NB]
        smat[1] = flat[:, NB:]

        def body(w, carry):
            re = smat[0, pl.ds(w, NTM * SEGS, stride=VPT), :]
            im = smat[1, pl.ds(w, NTM * SEGS, stride=VPT), :]
            real, imag = [], []
            for t in range(NTM):
                r, m = re[t * SEGS : (t + 1) * SEGS], im[t * SEGS : (t + 1) * SEGS]
                real += [r, m]
                imag += [-m, r]
            both = jnp.concatenate(real + imag, 0).T
            u[pl.ds(pl.multiple_of(2 * w * NB, NB), NB), 0:64] = both[:, :64]
            u[pl.ds(pl.multiple_of((2 * w + 1) * NB, NB), NB), 0:64] = both[:, 64:]
            return carry

        lax.fori_loop(0, VPT, body, 0)

    def whiten_channels(q):
        for d in range(1, NTM):
            energy(q, d, -1).wait_recv()
        total = ebuf[q, 0] + ebuf[q, 1] + ebuf[q, 2] + ebuf[q, 3]
        top = limit(jnp.sum(total, 0, keepdims=True))
        top = jnp.broadcast_to(top, (HALF, HALF)).T
        top = jnp.concatenate([top, top], 1)

        def body(s, carry):
            parts = []
            for j in range(4):
                y = ybuf[s * 4 + j].astype(F32)
                parts.append(jnp.clip(y, -top, top).astype(BF))
            sp = nt(fwd[...], jnp.concatenate(parts, 1))
            re, im = sp[:NB], sp[NB:]
            g = nn(grow[...], (re * re + im * im).astype(BF))
            scale = lax.rsqrt(g[:NB] * rcol[...] + g[NB:] * (0.1 / NB) + 1e-6)
            pbuf[pl.ds(s, NB, stride=16), :] = re * scale
            pbuf[pl.ds(8 + s, NB, stride=16), :] = im * scale
            return carry

        lax.fori_loop(0, SEGS, body, 0)
        zp[q] = pbuf[...].reshape(NB, 16, HALF).astype(BF)
        spread(q)

    def cross(q):
        def body(g, carry):
            for j in range(8):
                k = g * 8 + j
                lhs = u[pl.ds(k, 2 * VPT, stride=NB), :][:, :64].astype(BF)
                x[pl.ds(k, 2 * VPT, stride=NB), :] = nn(lhs, z[k, :, q * HALF : (q + 1) * HALF])
            return carry

        lax.fori_loop(0, NB // 8, body, 0)
        xout[:, :, q * HALF : (q + 1) * HALF] = x[...].reshape(VPT, 2 * NB, HALF).astype(BF)

    send_channels(0)
    arrive(2)
    halos_in(2)
    filter_sources()
    send_channels(1)
    whiten_sources()
    arrive(0)
    halos_in(0)
    filter_channels(0)
    whiten_channels(0)
    pass_on(0)
    arrive(1)
    halos_in(1)
    filter_channels(1)
    whiten_channels(1)
    sources_in()
    collect(0)
    pass_on(1)
    cross(0)
    collect(1)
    cross(1)

    for q in range(3):
        for d in range(1, NTM):
            energy(q, d, 1).wait_send()

        @pl.when(i < NTM - 1)
        def _():
            halo(q, 0).wait_send()

        @pl.when(i > 0)
        def _():
            halo(q, 1).wait_send()

        if q < 2:
            for h in range(2):
                direct(q, h, 0).wait_send()
                direct(q, h, 1).wait_send()
                forward(q, h).wait_send()
        if q > 0:

            def sent(d, carry, q=q):
                a2a(q, d, 1).wait_send()
                return carry

            lax.fori_loop(1, NBLK, sent, 0)

    for e in range(NTM):

        @pl.when((group != i) | (group != e))
        def _():
            source_copy(e).wait_send()


def cross_spectra(order, vs, raw, taps, fwd, grow, rcol, rrow):
    vm = pl.BlockSpec(memory_space=pltpu.VMEM)
    sm = pl.BlockSpec(memory_space=pltpu.SMEM)
    dma = pltpu.SemaphoreType.DMA
    return pl.pallas_call(
        spectra_kernel,
        out_shape=jax.ShapeDtypeStruct((VPT, 2 * NB, SLAB), BF),
        in_specs=[sm, sm, pl.BlockSpec(memory_space=pl.ANY), vm, vm, vm, vm, vm],
        out_specs=vm,
        scratch_shapes=[
            pltpu.VMEM((raw.shape[0], 2, 128), F32),
            pltpu.VMEM((2 * HALF, 128), F32),
            pltpu.VMEM((2, NBLK, HALF, SLAB), BF),
            pltpu.VMEM((VS, SLAB), BF),
            pltpu.VMEM((2, NBLK + 2, HALF, SLAB), BF),
            pltpu.VMEM((NBLK + 2, VPT, SLAB), BF),
            pltpu.VMEM((SLAB, 2 * SLAB), BF),
            pltpu.VMEM((NBLK, HALF, SLAB), BF),
            pltpu.VMEM((NBLK, VPT, SLAB), BF),
            pltpu.VMEM((NB * 16, HALF), F32),
            pltpu.VMEM((2, NB, 16, HALF), BF),
            pltpu.VMEM((NB, NTM * 16, SLAB), BF),
            pltpu.VMEM((SEGS, VPT, 2 * NB), BF),
            pltpu.VMEM((NTM, SEGS, VPT, 2 * NB), BF),
            pltpu.VMEM((2, NTM * SEGS * VPT, NB), F32),
            pltpu.VMEM((2 * VPT * NB, 128), F32),
            pltpu.VMEM((2 * VPT * NB, HALF), F32),
            pltpu.VMEM((2, NTM, 8, HALF), F32),
            pltpu.VMEM((NTM, VPT, 128), F32),
            dma((8,)), dma((3, NBLK)), dma((3, NBLK)), dma((3, 2)), dma((3, 2)),
            dma((3, NTM)), dma((3, NTM)), dma((2, 2, 3)), dma((2, 2, NTM)),
            dma((NTM,)), dma((NTM,)),
        ],
        compiler_params=pltpu.CompilerParams(
            collective_id=0, has_side_effects=True, vmem_limit_bytes=50 * MIB
        ),
    )(order, vs, raw, taps, fwd, grow, rcol, rrow)


def lag_kernel(x, inv, out):
    out[0] = tn(x[0], inv[...])


def lags(x, inv):
    return pl.pallas_call(
        lag_kernel,
        grid=(VPT,),
        in_specs=[
            pl.BlockSpec((1, 2 * NB, SLAB), lambda v: (v, 0, 0)),
            pl.BlockSpec((2 * NB, NF), lambda v: (0, 0)),
        ],
        out_specs=pl.BlockSpec((1, SLAB, NF), lambda v: (v, 0, 0)),
        out_shape=jax.ShapeDtypeStruct((VPT, SLAB, NF), F32),
        compiler_params=pltpu.CompilerParams(vmem_limit_bytes=32 * MIB),
    )(x, inv)


def on_device(raw_traces, fir_taps, chan_order, vs_index):
    fwd, inv, grow, rcount = tables()
    taps = jnp.broadcast_to(jnp.pad(fir_taps, (64, 2 * SLAB - 64 - TAPS))[None, :], (8, 2 * SLAB))
    x = cross_spectra(
        chan_order, vs_index, raw_traces, taps,
        jnp.asarray(fwd, BF), jnp.asarray(grow, BF),
        jnp.asarray(np.broadcast_to(rcount[:, None], (NB, HALF))),
        jnp.asarray(np.broadcast_to(rcount[None, :], (8, NB))),
    )
    return lags(x, jnp.asarray(inv, BF))


def solution(mesh):
    in_specs = (P(None, ("tm", "chan")), P(), P(), P())
    out_specs = P("tm", "chan", None)
    return jax.shard_map(
        on_device, mesh=mesh, in_specs=in_specs, out_specs=out_specs, check_vma=False
    )
```

time: 207 us -> 128 us (0.62); the launches traced: 203 us -> 127 us
  Pallas kernels: 194 us -> 122 us
    pallas_call x3 -> x2, Pallas kernels: 194 us -> 122 us  [the longest x1 111 us: cross_spectra(): pl.pallas_call(spectra_kernel, out_shape=jax.ShapeDtypeStruct((VPT, 2 * N...]
    unnamed x16 -> x10, local copies, waits for them, and re-layouts: 6.82 us -> 3.3 us
where the time goes in v2:
time: 128 us; the launch traced here: 127 us
  Pallas kernels  122 us (95%)
  local copies, waits for them, and re-layouts  5.5 us (4%)
    pallas_call x1, Pallas kernels, cross_spectra(): pl.pallas_call(spectra_kernel, out_shape=jax.ShapeDtypeStruct((VPT, 2 * N...  111 us
    pallas_call x1, Pallas kernels, lags(): pl.pallas_call(lag_kernel, grid=(VPT,), in_specs=[pl.BlockSpec((1, 2 * NB...  10.7 us
    unnamed x10, local copies, waits for them, and re-layouts  3.3 us

profile of v2, /device:TPU:2, one launch (start us, length us, event | category | flops | bytes accessed | tf_op | source)
XLA Modules:
  0.0 127.5 jit_solution(13326810380558584427)
XLA Ops:
  0.0 0.0 copy-start
  0.0 0.8 pad.4
  0.8 0.7 jit_solution_.7.rrow
  1.5 0.7 jit_solution_.6.rcol
  2.2 0.0 copy-start.1
  2.2 1.0 copy-done.1
  3.3 0.0 copy-start.2
  3.3 0.8 copy-done.2
  4.1 0.0 copy-start.3
  4.1 0.8 copy-done.3
  4.9 0.0 copy-start.4
  4.9 0.7 copy-done.4
  5.5 111.2 %shard_map.91.x = bf16[16,256,256]{2,1,0:T(8,128)(2,1)S(1)} custom-call(s32[8192]{0:T(1024)S(1)} %copy-done.3, s32[64]{0:T(128)S(1)} %copy-done.4, f32[8192,256]{1,0:T(8,128)} %raw.1, f32[8,512]{1,0:T(8,128)S(1)} %broadcast_in_dim.2.taps, bf16[256,1024]{1,0:T(8,128)(2,1)S(1)} %copy-done.1, bf16[256,128]{1,0:T(8,128)(2,1)S(1)} %copy-done.2, ...), custom_call_target="tpu_custom_call" | custom-call | tf_op jit(solution)/shard_map/pallas_call | solution.py:474
  116.7 0.0 copy-done
  116.7 10.7 %shard_map.92 = f32[16,256,1024]{2,1,0:T(8,128)} custom-call(bf16[16,256,256]{2,1,0:T(8,128)(2,1)S(1)} %shard_map.91.x, bf16[256,1024]{1,0:T(8,128)(2,1)S(1)} %copy-done), custom_call_target="tpu_custom_call" | custom-call | tf_op jit(solution)/shard_map/pallas_call | solution.py:514
  (1 shorter events, 0.0 us)
Async XLA Ops:
  0.0 116.7 %copy-start = (bf16[256,1024]{1,0:T(8,128)(2,1)S(1)}, bf16[256,1024]{1,0:T(8,128)(2,1)}, u32[]{:S(2)}) copy-start(bf16[256,1024]{1,0:T(8,128)(2,1)} %constant.14.clone.inv) | copy-start | bytes 1572868
  2.2 1.1 copy-start.1
  3.3 0.8 copy-start.2
  4.1 0.8 copy-start.3
  4.9 0.7 copy-start.4

commit v3 on v2

--- a/solution.py
+++ b/solution.py
@@ -20,7 +20,9 @@
 SEGS = 8
 VS = 64
 VPT = VS // NTM
-HALF = 128
+CHUNK = 64
+QN = SLAB // CHUNK
+HB = NB // 2
 T_ALL = SLAB * NBLK * NTM
 MIB = 1024 * 1024
 MESH = pl.DeviceIdType.MESH
@@ -36,13 +38,11 @@
     lag = (k * (n - NF // 2) % NF) * (2.0 * math.pi / NF)
     inv = np.concatenate([np.cos(lag), -np.sin(lag)], 0) / math.sqrt(SEGS * NTM * NB)
     near = np.abs(np.arange(NB)[:, None] - np.arange(NB)[None, :]) <= WS
-    count = near.sum(1)
     grow = np.concatenate([near, np.ones((NB, NB))], 0)
     return (
         fwd.astype(np.float32),
         inv.astype(np.float32),
         grow.astype(np.float32),
-        (1.0 / count).astype(np.float32),
     )
 
 
@@ -59,10 +59,10 @@
 
 
 def spectra_kernel(
-    order, vs, raw, taps, fwd, grow, rcol, rrow, xout,
-    rows2, line, send, srcs, recv, recvs, tt, ybuf, ysrc, pbuf, zp, z, sp_out, sg, smat, u, x,
+    order_in, vs_in, raw, taps_in, fwd_in, grow_in, xout,
+    order, vs, taps, fwd, grow, xs, rows2, line, send, srcs, recv, recvs, tt, ybuf, ysrc, pbuf, zp, z, sp_out, sg, smat, u, x,
     ebuf, esrc, r_sem, a_send, a_recv, h_send, h_recv, e_send, e_recv, g_send, g_recv,
-    s_send, s_recv,
+    s_send, s_recv, x_sem,
 ):
     i = lax.axis_index("tm")
     c = lax.axis_index("chan")
@@ -84,6 +84,16 @@
             raw.at[r, pl.ds((p % 2) * 128, 128)], rows2.at[r, p % 2], r_sem.at[p]
         )
 
+    small = [
+        pltpu.make_async_copy(a, b, r_sem.at[8 + n])
+        for n, (a, b) in enumerate(
+            (
+                (taps_in, taps), (order_in, order), (vs_in, vs), (fwd_in, fwd), (grow_in, grow),
+            )
+        )
+    ]
+    for copy in small:
+        copy.start()
     for p in range(8):
         load(p).start()
 
@@ -104,7 +114,15 @@
         def _():
             pl.semaphore_signal(barrier, inc=1, device_id=(t, base + i), device_id_type=MESH)
 
-    band = jnp.broadcast_to(taps[0:1, :], (SLAB, 2 * SLAB))
+    for copy in small:
+        copy.wait()
+    lane = lax.broadcasted_iota(jnp.int32, (1, 2 * SLAB), 1)
+
+    def tap(j, row):
+        return jnp.where(lane == j + 64, taps[j], row)
+
+    band = lax.fori_loop(0, TAPS, tap, jnp.zeros((1, 2 * SLAB), F32))
+    band = jnp.broadcast_to(band, (SLAB, 2 * SLAB))
     tt[...] = pltpu.roll(band, 0, 1, stride=1, stride_axis=0).astype(BF)
 
     for p in range(8):
@@ -122,7 +140,7 @@
     def a2a(q, d, sign):
         other = at_shift(d, sign)
         owner = c if sign > 0 else other
-        if q == 2:
+        if q == QN:
             src, dst = srcs.at[pl.ds((other % NTM) * VPT, VPT)], recvs.at[1 + owner]
         else:
             src, dst = send.at[q, d], recv.at[q, 1 + owner]
@@ -146,31 +164,39 @@
     srcs[:, 128:256] = hi
 
     def send_sources(d, carry):
-        a2a(2, d, 1).start()
+        a2a(QN, d, 1).start()
         return carry
 
     lax.fori_loop(1, NBLK, send_sources, 0)
     recvs[1 + c] = srcs[pl.ds(pl.multiple_of(group * VPT, VPT), VPT)]
 
-    def send_channels(q):
-        lo, hi = fetch(HALF, lambda r: order[c * SLAB + q * HALF + r])
+    def stage(q):
+        lo, hi = fetch(CHUNK, lambda r: order[c * SLAB + q * CHUNK + r])
         recv[q, 1 + c, :, 0:128] = lo
         recv[q, 1 + c, :, 128:256] = hi
 
         def body(d, carry):
-            start = at_shift(d, 1) * SLAB + q * HALF
-            lo, hi = fetch(HALF, lambda r: order[start + r])
+            first = at_shift(d, 1) * SLAB + q * CHUNK
+            lo, hi = fetch(CHUNK, lambda r: order[first + r])
             send[q, d, :, 0:128] = lo
             send[q, d, :, 128:256] = hi
-            if q == 1:
-                a2a(0, d, 1).wait_send()
+            if q == 0:
+                a2a(q, d, 1).start()
+            return carry
+
+        lax.fori_loop(1, NBLK, body, 0)
+
+    def send_channels(q, wait):
+        def body(d, carry):
+            if wait:
+                a2a(q - 1, d, 1).wait_send()
             a2a(q, d, 1).start()
             return carry
 
         lax.fori_loop(1, NBLK, body, 0)
 
     def box(q):
-        return recvs if q == 2 else recv.at[q]
+        return recvs if q == QN else recv.at[q]
 
     def halo(q, side):
         b = box(q)
@@ -193,7 +219,7 @@
 
         lax.fori_loop(1, NBLK, wait, 0)
         b = box(q)
-        rows = VPT if q == 2 else HALF
+        rows = VPT if q == QN else CHUNK
 
         @pl.when(i < NTM - 1)
         def _():
@@ -223,18 +249,18 @@
     def energy(q, d, sign):
         other = lax.rem(i + d, NTM)
         owner = i if sign > 0 else other
-        e = esrc if q == 2 else ebuf.at[q]
+        e = esrc if q == QN else ebuf.at[q]
         return pltpu.make_async_remote_copy(
             src_ref=e.at[owner], dst_ref=e.at[owner], send_sem=e_send.at[q, d],
             recv_sem=e_recv.at[q, owner], device_id=(other, c), device_id_type=MESH,
         )
 
     def block(q, h, owner):
-        return z.at[pl.ds(h * 64, 64), pl.ds(owner * 16, 16), pl.ds(q * HALF, HALF)]
+        return z.at[q, pl.ds(h * 32, 32), pl.ds(owner * 16, 16)]
 
     def direct(q, h, way):
         return pltpu.make_async_remote_copy(
-            src_ref=zp.at[q, pl.ds(h * 64, 64)], dst_ref=block(q, h, i),
+            src_ref=zp.at[q, pl.ds(h * 32, 32)], dst_ref=block(q, h, i),
             send_sem=g_send.at[q, h, way], recv_sem=g_recv.at[q, h, i],
             device_id=(up if way == 0 else down, c), device_id_type=MESH,
         )
@@ -259,7 +285,7 @@
             direct(q, h, h).start()
         for h in range(2):
             direct(q, h, 1 - h).start()
-        z[:, pl.ds(pl.multiple_of(i * 16, 16), 16), q * HALF : (q + 1) * HALF] = zp[q]
+        z[q, :, pl.ds(pl.multiple_of(i * 16, 16), 16)] = zp[q]
 
     def pass_on(q):
         for h in range(2):
@@ -286,27 +312,27 @@
         sq = sq[:, :128] + sq[:, 128:]
         esrc[i] = jnp.sum(sq.reshape(NBLK, VPT, 128), 0)
         for d in range(1, NTM):
-            energy(2, d, 1).start()
+            energy(QN, d, 1).start()
 
     def filter_channels(q):
         def body(g, acc):
-            b = g * 4
+            b = g * 8
             w = jnp.concatenate(
                 [
-                    recv[q, pl.ds(b, 4), :, 128:].reshape(4 * HALF, 128),
-                    recv[q, pl.ds(b + 1, 4)].reshape(4 * HALF, SLAB),
-                    recv[q, pl.ds(b + 2, 4), :, :128].reshape(4 * HALF, 128),
+                    recv[q, pl.ds(b, 8), :, 128:].reshape(8 * CHUNK, 128),
+                    recv[q, pl.ds(b + 1, 8)].reshape(8 * CHUNK, SLAB),
+                    recv[q, pl.ds(b + 2, 8), :, :128].reshape(8 * CHUNK, 128),
                 ],
                 1,
             )
             y = nt(w, tt[...])
-            ybuf[pl.ds(b, 4)] = y.astype(BF).reshape(4, HALF, SLAB)
+            ybuf[pl.ds(b, 8)] = y.astype(BF).reshape(8, CHUNK, SLAB)
             sq = y * y
             sq = sq[:, :128] + sq[:, 128:]
-            return acc + jnp.sum(sq.reshape(4, HALF, 128), 0)
-
-        acc = lax.fori_loop(0, NBLK // 4, body, jnp.zeros((HALF, 128), F32))
-        ebuf[q, i] = jnp.sum(acc.T.reshape(16, 8, HALF), 0)
+            return acc + jnp.sum(sq.reshape(8, CHUNK, 128), 0)
+
+        acc = lax.fori_loop(0, NBLK // 8, body, jnp.zeros((CHUNK, 128), F32))
+        ebuf[q, i] = jnp.sum(jnp.concatenate([acc, acc], 0).T.reshape(16, 8, 2 * CHUNK), 0)
         for d in range(1, NTM):
             energy(q, d, 1).start()
 
@@ -325,9 +351,15 @@
             device_id=(t, base + i), device_id_type=MESH,
         )
 
+    def per_bin(axis):
+        k = lax.broadcasted_iota(jnp.int32, (NB, NB) if axis == 0 else (8, NB), axis)
+        count = jnp.minimum(k + WS, NB - 1) - jnp.maximum(k - WS, 0) + 1
+        inverse_count = 1.0 / count.astype(F32)
+        return inverse_count if axis == 0 else inverse_count[0:1, :]
+
     def whiten_sources():
         for d in range(1, NTM):
-            energy(2, d, -1).wait_recv()
+            energy(QN, d, -1).wait_recv()
         total = esrc[0] + esrc[1] + esrc[2] + esrc[3]
         top = limit(jnp.sum(total, 1, keepdims=True))
         top = jnp.broadcast_to(top[None], (SEGS, VPT, 1)).reshape(SEGS * VPT, 1)
@@ -338,7 +370,7 @@
         sp = nt(jnp.concatenate(parts, 1), fwd[...])
         re, im = sp[:, :NB], sp[:, NB:]
         g = nt((re * re + im * im).astype(BF), grow[...])
-        scale = lax.rsqrt(g[:, :NB] * rrow[0:1, :] + g[:, NB:] * (0.1 / NB) + 1e-6)
+        scale = lax.rsqrt(g[:, :NB] * per_bin(1) + g[:, NB:] * (0.1 / NB) + 1e-6)
         white = jnp.concatenate([re * scale, im * scale], 1).astype(BF)
         sp_out[...] = white.reshape(SEGS, VPT, 2 * NB)
         for e in range(NTM):
@@ -375,67 +407,124 @@
             u[pl.ds(pl.multiple_of((2 * w + 1) * NB, NB), NB), 0:64] = both[:, 64:]
             return carry
 
-        lax.fori_loop(0, VPT, body, 0)
+        lax.fori_loop(0, VPT, body, 0, unroll=4)
 
     def whiten_channels(q):
         for d in range(1, NTM):
             energy(q, d, -1).wait_recv()
         total = ebuf[q, 0] + ebuf[q, 1] + ebuf[q, 2] + ebuf[q, 3]
         top = limit(jnp.sum(total, 0, keepdims=True))
-        top = jnp.broadcast_to(top, (HALF, HALF)).T
+        top = jnp.broadcast_to(top, (128, 128)).T[0:CHUNK]
         top = jnp.concatenate([top, top], 1)
-
-        def body(s, carry):
+        low = lax.broadcasted_iota(jnp.int32, (HB, 128), 1) < CHUNK
+
+        def body(t, carry):
             parts = []
             for j in range(4):
-                y = ybuf[s * 4 + j].astype(F32)
-                parts.append(jnp.clip(y, -top, top).astype(BF))
+                two = []
+                for s in range(2):
+                    y = ybuf[(2 * t + s) * 4 + j].astype(F32)
+                    two.append(jnp.clip(y, -top, top).astype(BF))
+                parts.append(jnp.concatenate(two, 0))
             sp = nt(fwd[...], jnp.concatenate(parts, 1))
             re, im = sp[:NB], sp[NB:]
             g = nn(grow[...], (re * re + im * im).astype(BF))
-            scale = lax.rsqrt(g[:NB] * rcol[...] + g[NB:] * (0.1 / NB) + 1e-6)
-            pbuf[pl.ds(s, NB, stride=16), :] = re * scale
-            pbuf[pl.ds(8 + s, NB, stride=16), :] = im * scale
-            return carry
-
-        lax.fori_loop(0, SEGS, body, 0)
-        zp[q] = pbuf[...].reshape(NB, 16, HALF).astype(BF)
+            scale = lax.rsqrt(g[:NB] * per_bin(0) + g[NB:] * (0.1 / NB) + 1e-6)
+            for n, part in enumerate((re * scale, im * scale)):
+                turned = pltpu.roll(part, CHUNK, 1)
+                first = jnp.where(low, part[:HB], turned[HB:])
+                second = jnp.where(low, turned[:HB], part[HB:])
+                pbuf[pl.ds(n * SEGS + 2 * t, HB, stride=16), :] = first
+                pbuf[pl.ds(n * SEGS + 2 * t + 1, HB, stride=16), :] = second
+            return carry
+
+        lax.fori_loop(0, SEGS // 2, body, 0, unroll=2)
+        zp[q] = pbuf[...].reshape(HB, 16, 128).astype(BF)
         spread(q)
 
     def cross(q):
         def body(g, carry):
-            for j in range(8):
-                k = g * 8 + j
-                lhs = u[pl.ds(k, 2 * VPT, stride=NB), :][:, :64].astype(BF)
-                x[pl.ds(k, 2 * VPT, stride=NB), :] = nn(lhs, z[k, :, q * HALF : (q + 1) * HALF])
-            return carry
-
-        lax.fori_loop(0, NB // 8, body, 0)
-        xout[:, :, q * HALF : (q + 1) * HALF] = x[...].reshape(VPT, 2 * NB, HALF).astype(BF)
-
-    send_channels(0)
-    arrive(2)
-    halos_in(2)
+            for j in range(16):
+                k = g * 16 + j
+                lhs = u[pl.ds(k, 4 * VPT, stride=HB), :][:, :64].astype(BF)
+                x[q % 2, pl.ds(k, 4 * VPT, stride=HB), :] = nn(lhs, z[q, k])
+            return carry
+
+        lax.fori_loop(0, HB // 16, body, 0)
+
+    def leave(p, g):
+        part = pl.ds(2 * g, 2)
+        return pltpu.make_async_copy(xs.at[p, part], xout.at[p, part], x_sem.at[p, g])
+
+    def merge(p):
+        low = lax.broadcasted_iota(jnp.int32, (HB, 128), 1) < CHUNK
+
+        def body(g, carry):
+            done = []
+            for t in range(4):
+                for kh in range(2):
+                    rows = pl.ds(pl.multiple_of(g * (4 * NB) + t * NB + kh * HB, HB), HB)
+                    even, odd = x[0, rows, :], x[1, rows, :]
+                    if kh == 0:
+                        both = jnp.where(low, even, pltpu.roll(odd, CHUNK, 1))
+                    else:
+                        both = jnp.where(low, pltpu.roll(even, CHUNK, 1), odd)
+                    done.append((t, kh, both.astype(BF)))
+            for t, kh, both in done:
+                k0 = (t % 2) * NB + kh * HB
+                xs[p, 2 * g + t // 2, k0 : k0 + HB] = both
+            leave(p, g).start()
+            return carry
+
+        lax.fori_loop(0, VPT // 2, body, 0)
+
+    stage(0)
+    arrive(QN)
+    stage(1)
+    send_channels(1, True)
+    halos_in(QN)
     filter_sources()
-    send_channels(1)
+    arrive(0)
+    stage(2)
     whiten_sources()
-    arrive(0)
     halos_in(0)
     filter_channels(0)
+    sources_in()
     whiten_channels(0)
-    pass_on(0)
+    send_channels(2, False)
     arrive(1)
+    stage(3)
     halos_in(1)
     filter_channels(1)
+    pass_on(0)
     whiten_channels(1)
-    sources_in()
+    send_channels(3, False)
+    arrive(2)
     collect(0)
+    cross(0)
+    halos_in(2)
+    filter_channels(2)
     pass_on(1)
-    cross(0)
+    whiten_channels(2)
+    arrive(3)
     collect(1)
     cross(1)
-
-    for q in range(3):
+    halos_in(3)
+    filter_channels(3)
+    pass_on(2)
+    merge(0)
+    whiten_channels(3)
+    collect(2)
+    cross(2)
+    pass_on(3)
+    collect(3)
+    cross(3)
+    merge(1)
+
+    for p in range(2):
+        for g in range(VPT // 2):
+            leave(p, g).wait()
+    for q in range(QN + 1):
         for d in range(1, NTM):
             energy(q, d, 1).wait_send()
 
@@ -447,7 +536,7 @@
         def _():
             halo(q, 1).wait_send()
 
-        if q < 2:
+        if q < QN:
             for h in range(2):
                 direct(q, h, 0).wait_send()
                 direct(q, h, 1).wait_send()
@@ -467,71 +556,95 @@
             source_copy(e).wait_send()
 
 
-def cross_spectra(order, vs, raw, taps, fwd, grow, rcol, rrow):
-    vm = pl.BlockSpec(memory_space=pltpu.VMEM)
-    sm = pl.BlockSpec(memory_space=pltpu.SMEM)
+def cross_spectra(order, vs, raw, taps, fwd, grow):
+    hb = pl.BlockSpec(memory_space=pl.ANY)
     dma = pltpu.SemaphoreType.DMA
     return pl.pallas_call(
         spectra_kernel,
-        out_shape=jax.ShapeDtypeStruct((VPT, 2 * NB, SLAB), BF),
-        in_specs=[sm, sm, pl.BlockSpec(memory_space=pl.ANY), vm, vm, vm, vm, vm],
-        out_specs=vm,
+        out_shape=jax.ShapeDtypeStruct((2, VPT, 2 * NB, 128), BF),
+        in_specs=[hb] * 6,
+        out_specs=hb,
         scratch_shapes=[
+            pltpu.SMEM(order.shape, jnp.int32),
+            pltpu.SMEM(vs.shape, jnp.int32),
+            pltpu.SMEM(taps.shape, F32),
+            pltpu.VMEM(fwd.shape, BF),
+            pltpu.VMEM(grow.shape, BF),
+            pltpu.VMEM((2, VPT, 2 * NB, 128), BF),
             pltpu.VMEM((raw.shape[0], 2, 128), F32),
-            pltpu.VMEM((2 * HALF, 128), F32),
-            pltpu.VMEM((2, NBLK, HALF, SLAB), BF),
+            pltpu.VMEM((2 * CHUNK, 128), F32),
+            pltpu.VMEM((QN, NBLK, CHUNK, SLAB), BF),
             pltpu.VMEM((VS, SLAB), BF),
-            pltpu.VMEM((2, NBLK + 2, HALF, SLAB), BF),
+            pltpu.VMEM((QN, NBLK + 2, CHUNK, SLAB), BF),
             pltpu.VMEM((NBLK + 2, VPT, SLAB), BF),
             pltpu.VMEM((SLAB, 2 * SLAB), BF),
-            pltpu.VMEM((NBLK, HALF, SLAB), BF),
+            pltpu.VMEM((NBLK, CHUNK, SLAB), BF),
             pltpu.VMEM((NBLK, VPT, SLAB), BF),
-            pltpu.VMEM((NB * 16, HALF), F32),
-            pltpu.VMEM((2, NB, 16, HALF), BF),
-            pltpu.VMEM((NB, NTM * 16, SLAB), BF),
+            pltpu.VMEM((HB * 16, 128), F32),
+            pltpu.VMEM((QN, HB, 16, 128), BF),
+            pltpu.VMEM((QN, HB, NTM * 16, 128), BF),
             pltpu.VMEM((SEGS, VPT, 2 * NB), BF),
             pltpu.VMEM((NTM, SEGS, VPT, 2 * NB), BF),
             pltpu.VMEM((2, NTM * SEGS * VPT, NB), F32),
             pltpu.VMEM((2 * VPT * NB, 128), F32),
-            pltpu.VMEM((2 * VPT * NB, HALF), F32),
-            pltpu.VMEM((2, NTM, 8, HALF), F32),
+            pltpu.VMEM((2, 2 * VPT * NB, 128), F32),
+            pltpu.VMEM((QN, NTM, 8, 128), F32),
             pltpu.VMEM((NTM, VPT, 128), F32),
-            dma((8,)), dma((3, NBLK)), dma((3, NBLK)), dma((3, 2)), dma((3, 2)),
-            dma((3, NTM)), dma((3, NTM)), dma((2, 2, 3)), dma((2, 2, NTM)),
-            dma((NTM,)), dma((NTM,)),
+            dma((13,)), dma((QN + 1, NBLK)), dma((QN + 1, NBLK)),
+            dma((QN + 1, 2)), dma((QN + 1, 2)), dma((QN + 1, NTM)), dma((QN + 1, NTM)),
+            dma((QN, 2, 3)), dma((QN, 2, NTM)), dma((NTM,)), dma((NTM,)), dma((2, VPT // 2)),
         ],
         compiler_params=pltpu.CompilerParams(
-            collective_id=0, has_side_effects=True, vmem_limit_bytes=50 * MIB
+            collective_id=0, has_side_effects=True, vmem_limit_bytes=56 * MIB
         ),
-    )(order, vs, raw, taps, fwd, grow, rcol, rrow)
-
-
-def lag_kernel(x, inv, out):
-    out[0] = tn(x[0], inv[...])
+    )(order, vs, raw, taps, fwd, grow)
+
+
+SLOTS = 4
+
+
+def lag_kernel(x, inv, out, xb, buf, in_sem, sem):
+    def enter(v):
+        return pltpu.make_async_copy(x.at[:, v], xb.at[:, v], in_sem.at[v])
+
+    def leave(v):
+        return pltpu.make_async_copy(buf.at[v % SLOTS], out.at[v], sem.at[v % SLOTS])
+
+    for v in range(VPT):
+        enter(v).start()
+    for v in range(VPT):
+        enter(v).wait()
+        if v >= SLOTS:
+            leave(v - SLOTS).wait()
+        for h in range(2):
+            rows = slice(h * 128, h * 128 + 128)
+            buf[v % SLOTS, rows] = tn(xb[h, v], inv[...])
+        leave(v).start()
+    for v in range(VPT - SLOTS, VPT):
+        leave(v).wait()
 
 
 def lags(x, inv):
     return pl.pallas_call(
         lag_kernel,
-        grid=(VPT,),
-        in_specs=[
-            pl.BlockSpec((1, 2 * NB, SLAB), lambda v: (v, 0, 0)),
-            pl.BlockSpec((2 * NB, NF), lambda v: (0, 0)),
+        in_specs=[pl.BlockSpec(memory_space=pl.ANY), pl.BlockSpec(memory_space=pltpu.VMEM)],
+        out_specs=pl.BlockSpec(memory_space=pl.ANY),
+        out_shape=jax.ShapeDtypeStruct((VPT, SLAB, NF), F32),
+        scratch_shapes=[
+            pltpu.VMEM((2, VPT, 2 * NB, 128), BF),
+            pltpu.VMEM((SLOTS, SLAB, NF), F32),
+            pltpu.SemaphoreType.DMA((VPT,)),
+            pltpu.SemaphoreType.DMA((SLOTS,)),
         ],
-        out_specs=pl.BlockSpec((1, SLAB, NF), lambda v: (v, 0, 0)),
-        out_shape=jax.ShapeDtypeStruct((VPT, SLAB, NF), F32),
-        compiler_params=pltpu.CompilerParams(vmem_limit_bytes=32 * MIB),
+        compiler_params=pltpu.CompilerParams(vmem_limit_bytes=60 * MIB),
     )(x, inv)
 
 
 def on_device(raw_traces, fir_taps, chan_order, vs_index):
-    fwd, inv, grow, rcount = tables()
-    taps = jnp.broadcast_to(jnp.pad(fir_taps, (64, 2 * SLAB - 64 - TAPS))[None, :], (8, 2 * SLAB))
+    fwd, inv, grow = tables()
     x = cross_spectra(
-        chan_order, vs_index, raw_traces, taps,
+        chan_order, vs_index, raw_traces, fir_taps,
         jnp.asarray(fwd, BF), jnp.asarray(grow, BF),
-        jnp.asarray(np.broadcast_to(rcount[:, None], (NB, HALF))),
-        jnp.asarray(np.broadcast_to(rcount[None, :], (8, NB))),
     )
     return lags(x, jnp.asarray(inv, BF))
 

time: 128 us -> 114 us (0.89)
  Pallas kernels: 122 us -> 113 us
  local copies, waits for them, and re-layouts: 5.5 us -> 0 us
    pallas_call x2, Pallas kernels: 122 us -> 113 us  [the longest x1 104 us: cross_spectra(): pl.pallas_call(spectra_kernel, out_shape=jax.ShapeDtypeStruct((2, VPT, 2...]
    unnamed x10 -> x0, local copies, waits for them, and re-layouts: 3.3 us -> none
    another operation x2 -> x0, local copies, waits for them, and re-layouts: 1.38 us -> none
where the time goes in v3:
time: 114 us; the launch traced here: 113 us
  Pallas kernels  113 us (99%)
    pallas_call x1, Pallas kernels, cross_spectra(): pl.pallas_call(spectra_kernel, out_shape=jax.ShapeDtypeStruct((2, VPT, 2...  104 us
    pallas_call x1, Pallas kernels, lags(): pl.pallas_call(lag_kernel, in_specs=[pl.BlockSpec(memory_space=pl.ANY), p...  8.44 us

profile of v3, /device:TPU:2, one launch (start us, length us, event | category | flops | bytes accessed | tf_op | source)
XLA Modules:
  0.0 112.8 jit_solution(14476332294916269119)
XLA Ops:
  0.0 104.1 %shard_map.73.x = bf16[2,16,256,128]{3,2,1,0:T(8,128)(2,1)} custom-call(s32[8192]{0:T(1024)} %order_in.1, s32[64]{0:T(128)} %vs_in.1, f32[8192,256]{1,0:T(8,128)} %raw.1, f32[129]{0:T(256)} %taps_in.1, bf16[256,1024]{1,0:T(8,128)(2,1)} %constant.6.clone.fwd_in, bf16[256,128]{1,0:T(8,128)(2,1)} %constant.7.clone.grow_in), custom_call_target="tpu_custom_call" | custom-call | tf_op jit(solution)/shard_map/pallas_call | solution.py:562
  104.2 8.4 %shard_map.74 = f32[16,256,1024]{2,1,0:T(8,128)} custom-call(bf16[2,16,256,128]{3,2,1,0:T(8,128)(2,1)} %shard_map.73.x, bf16[256,1024]{1,0:T(8,128)(2,1)} %constant.8.clone.inv), custom_call_target="tpu_custom_call" | custom-call | tf_op jit(solution)/shard_map/pallas_call | solution.py:628

commit v4 on v3

--- a/solution.py
+++ b/solution.py
@@ -71,7 +71,7 @@
     up, down = lax.rem(i + 1, NTM), lax.rem(i + NTM - 1, NTM)
 
     def at_shift(d, sign):
-        d = (d * 11) % NBLK
+        d = (d * 13) % NBLK
         z = lax.rem(cz + sign * (d // 8) + 4, 4)
         x = lax.rem(cx + sign * ((d // 2) % 4) + 4, 4)
         k = lax.rem(cc + d % 2, 2)
@@ -186,14 +186,13 @@
 
         lax.fori_loop(1, NBLK, body, 0)
 
-    def send_channels(q, wait):
+    def send_channels(q, first, stop):
         def body(d, carry):
-            if wait:
-                a2a(q - 1, d, 1).wait_send()
+            a2a(q - 1, d, 1).wait_send()
             a2a(q, d, 1).start()
             return carry
 
-        lax.fori_loop(1, NBLK, body, 0)
+        lax.fori_loop(first, stop, body, 0)
 
     def box(q):
         return recvs if q == QN else recv.at[q]
@@ -481,24 +480,31 @@
     stage(0)
     arrive(QN)
     stage(1)
-    send_channels(1, True)
+    send_channels(1, 1, 16)
     halos_in(QN)
     filter_sources()
+    send_channels(1, 16, NBLK)
     arrive(0)
     stage(2)
-    whiten_sources()
+    send_channels(2, 1, 11)
     halos_in(0)
     filter_channels(0)
-    sources_in()
+    send_channels(2, 11, 18)
     whiten_channels(0)
-    send_channels(2, False)
+    send_channels(2, 18, 26)
+    whiten_sources()
+    send_channels(2, 26, NBLK)
     arrive(1)
     stage(3)
+    send_channels(3, 1, 11)
     halos_in(1)
     filter_channels(1)
     pass_on(0)
+    send_channels(3, 11, 18)
     whiten_channels(1)
-    send_channels(3, False)
+    send_channels(3, 18, 26)
+    sources_in()
+    send_channels(3, 26, NBLK)
     arrive(2)
     collect(0)
     cross(0)
@@ -541,7 +547,7 @@
                 direct(q, h, 0).wait_send()
                 direct(q, h, 1).wait_send()
                 forward(q, h).wait_send()
-        if q > 0:
+        if q >= QN - 1:
 
             def sent(d, carry, q=q):
                 a2a(q, d, 1).wait_send()

time: 114 us -> 110 us (0.965)
  the two profiles are of different devices: /device:TPU:2 before, /device:TPU:40 now
where the time goes in v4:
time: 110 us
  Pallas kernels  109 us (99%)
    pallas_call x1, Pallas kernels, cross_spectra(): pl.pallas_call(spectra_kernel, out_shape=jax.ShapeDtypeStruct((2, VPT, 2...  101 us
    pallas_call x1, Pallas kernels, lags(): pl.pallas_call(lag_kernel, in_specs=[pl.BlockSpec(memory_space=pl.ANY), p...  8.45 us

profile of v4, /device:TPU:40, one launch (start us, length us, event | category | flops | bytes accessed | tf_op | source)
XLA Modules:
  0.0 109.5 jit_solution(6779474062379754031)
XLA Ops:
  0.0 100.9 %shard_map.73.x = bf16[2,16,256,128]{3,2,1,0:T(8,128)(2,1)} custom-call(s32[8192]{0:T(1024)} %order_in.1, s32[64]{0:T(128)} %vs_in.1, f32[8192,256]{1,0:T(8,128)} %raw.1, f32[129]{0:T(256)} %taps_in.1, bf16[256,1024]{1,0:T(8,128)(2,1)} %constant.6.clone.fwd_in, bf16[256,128]{1,0:T(8,128)(2,1)} %constant.7.clone.grow_in), custom_call_target="tpu_custom_call" | custom-call | tf_op jit(solution)/shard_map/pallas_call | solution.py:568
  100.9 8.5 %shard_map.74 = f32[16,256,1024]{2,1,0:T(8,128)} custom-call(bf16[2,16,256,128]{3,2,1,0:T(8,128)(2,1)} %shard_map.73.x, bf16[256,1024]{1,0:T(8,128)(2,1)} %constant.8.clone.inv), custom_call_target="tpu_custom_call" | custom-call | tf_op jit(solution)/shard_map/pallas_call | solution.py:634
